TPU v7x, 512 devices: a whole 4x8x8 slice. The times are simulated.
512 devices in a mesh: dp: 64 (over z, y_hi, core), blk: 8 (over x, y_lo).
Axes of the slice: x: 4, y: 8 (y_hi: 4, y_lo: 2; y = y_hi * 2 + y_lo), z: 8, core: 2. Of those that a mesh axis runs over, the one named last changes fastest.
Arguments:
- activations: bfloat16 [40960, 3584], P('dp'), may hold values from -16 to 16
Outputs:
- factor_blocks: float32 [512, 16384], P('dp', 'blk')
All inputs are finite; a program needn't handle non-finite values.
Results may differ from a plain program's by a relative error of at most 0.0003.
Values sent between devices are 32-bit elements; how exact they have to be, the bound alone decides.
No kernel may reach another device: no remote copies, remote signals or barrier semaphores. Data moves between devices by JAX's collectives and lax.ppermute only.
A program may use at most 64 MiB of HBM per device.

v0:
```python
import jax
import jax.numpy as jnp
import numpy as np
from jax import lax
from jax.sharding import PartitionSpec as P

BS = 512


DAMPING = 0.1


def from_root(value, axis, source):
    kept = jnp.where(lax.axis_index(axis) == source, value, 0).astype(value.dtype)
    return lax.psum(kept, axis)


def block_tables(count, owners):
    pair_list = [(i, j) for j in range(count) for i in range(j, count)]
    slot_count = (len(pair_list) + owners - 1) // owners
    panel_count = (count + owners - 1) // owners
    tables = np.zeros((5, owners, slot_count), np.int32)
    for owner in range(owners):
        for slot in range(slot_count):
            index = slot * owners + owner
            if index < len(pair_list):
                i, j = pair_list[index]
                tables[0, owner, slot] = i
                tables[1, owner, slot] = j
                tables[2, owner, slot] = 1
                tables[3, owner, slot] = i % owners * panel_count + i // owners
                tables[4, owner, slot] = j % owners * panel_count + j // owners
    return (tables, slot_count, panel_count)


def body(activations):
    n_dp = lax.axis_size("dp")
    n_blk = lax.axis_size("blk")
    owner = lax.axis_index("blk")
    row_group = lax.axis_index("dp")
    tok_rows, order = activations.shape
    nblocks = order // BS
    row_count = BS // n_dp
    tables, slot_count, panel_count = block_tables(nblocks, n_blk)
    chosen = jnp.asarray(tables, jnp.int32)[:, owner, :]
    block_row = chosen[0]
    block_col = chosen[1]
    live_slot = chosen[2] == 1
    row_pos = chosen[3]
    col_pos = chosen[4]
    as_blocks = activations.reshape(tok_rows, nblocks, BS)
    left_cols = as_blocks[:, block_row, :]
    right_cols = as_blocks[:, block_col, :]
    term = jnp.einsum("tkr,tkc->rkc", left_cols, right_cols, preferred_element_type=jnp.float32)
    summed = lax.psum_scatter(
        term.reshape(row_count * lax.axis_size("dp"), slot_count * BS),
        "dp",
        scatter_dimension=0,
        tiled=True,
    )
    local_rows = summed.reshape(row_count, slot_count, BS) / (tok_rows * n_dp)
    global_row = row_group * row_count + lax.broadcasted_iota(jnp.int32, (row_count, BS), 0)
    column_ids = lax.broadcasted_iota(jnp.int32, (row_count, BS), 1)
    on_diagonal = jnp.where(global_row == column_ids, DAMPING, 0.0).astype(jnp.float32)
    diag_slot = jnp.where((block_row == block_col) & live_slot, 1.0, 0.0).astype(jnp.float32)
    local_rows = local_rows + on_diagonal[:, None, :] * diag_slot[None, :, None]
    whole_slab = lax.all_gather(local_rows[:, 0, :], "dp", axis=0, tiled=True)
    diag_block = from_root(whole_slab, "blk", 0)
    corner = jnp.linalg.cholesky(diag_block)
    identity = jnp.eye(BS, dtype=jnp.float32)
    corner_inverse = lax.linalg.triangular_solve(corner, identity, left_side=True, lower=True)
    solved = jnp.einsum("rkc,dc->rkd", local_rows, corner_inverse, precision=lax.Precision.HIGHEST)
    own_corner = lax.dynamic_slice_in_dim(corner, row_group * row_count, row_count, 0)
    first_column = (block_col == 0) & live_slot
    is_corner = first_column & (block_row == 0)
    panel_rows = jnp.where(is_corner[None, :, None], own_corner[:, None, :], solved)
    panel_rows = jnp.where(first_column[None, :, None], panel_rows, 0.0)
    panel_piece = panel_rows[:, :panel_count, :]
    by_rows = lax.all_gather(panel_piece, "dp", axis=0, tiled=True)
    full_panel = lax.all_gather(by_rows, "blk", axis=1, tiled=True)
    own_panel = lax.dynamic_slice_in_dim(full_panel, row_group * row_count, row_count, 0)
    left_panel = own_panel[:, row_pos, :]
    right_panel = full_panel[:, col_pos, :]
    update = jnp.einsum("rkd,ckd->rkc", left_panel, right_panel, precision=lax.Precision.HIGHEST)
    trailing = local_rows - update
    result = jnp.where(first_column[None, :, None], panel_rows, trailing)
    result = jnp.where(live_slot[None, :, None], result, 0.0)
    return result.reshape(row_count, slot_count * BS)


def solution(mesh):
    in_specs = (P("dp", None),)
    out_specs = P("dp", "blk")
    return jax.shard_map(body, mesh=mesh, in_specs=in_specs, out_specs=out_specs, check_vma=False)
```

profile of v0, /device:TPU:1, one launch (start us, length us, event | category | flops | bytes accessed | tf_op | source)
XLA Modules:
  0.0 799.4 jit_solution(13902125347907995900)
XLA Ops:
  6.5 7.2 copy.43
  13.8 7.3 copy.44
  21.8 3.0 gather_fusion
  24.8 4.6 gather_fusion.1
  29.4 5.5 fusion.2
  34.9 5.4 copy.55
  42.4 155.3 %reduce-scatter.4.cloned.1.call-done = f32[8,2048]{1,0:T(8,128)} async-done(((f32[512,2048]{1,0:T(8,128)}), f32[8,2048]{1,0:T(8,128)}) %reduce-scatter.4.cloned.1.call-update) | async-done | bytes 65552 | tf_op jit(solution)/shard_map/reduce_scatter | solution.py:55
  199.4 86.6 %all-gather.9.cloned.1.call-done = f32[512,1,512]{2,1,0:T(1,128)} async-done(((f32[8,1,512]{2,1,0:T(1,128)}), f32[512,1,512]{2,1,0:T(1,128)}) %all-gather.9.cloned.1.call-update) | async-done | bytes 1048592 | tf_op jit(solution)/shard_map/all_gather | solution.py:67
  286.0 2.3 copy.50
  291.5 80.3 %all-reduce.3.cloned.1.call-done = f32[512,512]{0,1:T(8,128)} async-done(((f32[512,512]{0,1:T(8,128)}), f32[512,512]{0,1:T(8,128)}) %all-reduce.3.cloned.1.call-update) | async-done | bytes 1048592 | tf_op jit(solution)/shard_map/psum | solution.py:15
  371.8 1.6 copy.51
  373.4 1.4 fusion.24
  374.8 11.7 %cholesky.103 = f32[128,128]{1,0:T(8,128)S(1)} custom-call(f32[128,128]{1,0:T(8,128)S(1)} %cholesky.263), custom_call_target="Cholesky" | custom-call | tf_op jit(solution)/shard_map/jit(cholesky)/cholesky | solution.py:69
  387.2 9.8 %custom-call.30 = f32[1,128,128]{1,2,0:T(8,128)S(1)} custom-call(f32[1,128,128]{2,1,0:T(8,128)S(1)} %get-tuple-element.37), custom_call_target="InvertDiagBlocksLowerTriangular" | custom-call | tf_op jit(solution)/shard_map/jit(cholesky)/cholesky | solution.py:69
  397.7 11.7 %cholesky.215 = f32[128,128]{1,0:T(8,128)S(1)} custom-call(f32[128,128]{1,0:T(8,128)S(1)} %cholesky.267), custom_call_target="Cholesky" | custom-call | tf_op jit(solution)/shard_map/jit(cholesky)/cholesky | solution.py:69
  410.1 1.4 compare_reduce_fusion.3
  411.5 10.0 %custom-call.31 = f32[1,128,128]{1,2,0:T(8,128)S(1)} custom-call(f32[1,128,128]{2,1,0:T(8,128)S(1)} %get-tuple-element.34), custom_call_target="InvertDiagBlocksLowerTriangular" | custom-call | tf_op jit(solution)/shard_map/jit(cholesky)/cholesky | solution.py:69
  422.1 11.7 %cholesky.236 = f32[128,128]{1,0:T(8,128)S(1)} custom-call(f32[128,128]{1,0:T(8,128)S(1)} %cholesky.272), custom_call_target="Cholesky" | custom-call | tf_op jit(solution)/shard_map/jit(cholesky)/cholesky | solution.py:69
  434.5 9.8 %custom-call.32 = f32[1,128,128]{1,2,0:T(8,128)S(1)} custom-call(f32[1,128,128]{2,1,0:T(8,128)S(1)} %get-tuple-element.31), custom_call_target="InvertDiagBlocksLowerTriangular" | custom-call | tf_op jit(solution)/shard_map/jit(cholesky)/cholesky | solution.py:69
  444.9 11.9 %cholesky.253 = f32[128,128]{1,0:T(8,128)S(1)} custom-call(f32[128,128]{1,0:T(8,128)S(1)} %convolution_subtract_fusion.5), custom_call_target="Cholesky" | custom-call | tf_op jit(solution)/shard_map/jit(cholesky)/cholesky | solution.py:69
  460.1 1.3 fusion.25
  461.9 10.9 %while.1 = (s32[]{:T(128)}, f32[512,512]{1,0:T(8,128)S(1)}, s32[4,2]{0,1:T(2,128)S(1)}, f32[4,128,128]{2,1,0:T(8,128)}, s32[]{:T(128)}) while((s32[]{:T(128)}, f32[512,512]{1,0:T(8,128)S(1)}, s32[4,2]{0,1:T(2,128)S(1)}, f32[4,128,128]{2,1,0:T(8,128)}, s32[]{:T(128)}) %tuple.34), condition=%wide.while_cond, body=%wide.while_body.sunk | while | flops 2 | bytes 132705 | solution.py:71
  462.6 2.0 bitcast_dynamic-update-slice_fusion.2
  465.3 2.1 bitcast_dynamic-update-slice_fusion.2
  468.0 2.0 bitcast_dynamic-update-slice_fusion.2
  470.8 2.0 bitcast_dynamic-update-slice_fusion.2
  472.8 40.1 %custom-call.33 = f32[4,128,128]{1,2,0:T(8,128)S(1)} custom-call(f32[4,128,128]{2,1,0:T(8,128)} %get-tuple-element.12), custom_call_target="InvertDiagBlocksLowerTriangular" | custom-call | tf_op jit(solution)/shard_map/triangular_solve | solution.py:71
  519.3 87.2 %all-gather.5.cloned.1.call-done = f32[512,1,512]{2,1,0:T(1,128)} async-done(((f32[8,1,512]{2,1,0:T(1,128)}), f32[512,1,512]{2,1,0:T(1,128)}) %all-gather.5.cloned.1.call-update) | async-done | bytes 1048592 | tf_op jit(solution)/shard_map/all_gather | solution.py:79
  606.5 2.4 copy.53
  608.9 169.7 %all-gather.7.cloned.1.call-done = f32[512,8,512]{2,0,1:T(8,128)} async-done(((f32[512,1,512]{2,0,1:T(8,128)}), f32[512,8,512]{2,0,1:T(8,128)}) %all-gather.7.cloned.1.call-update) | async-done | bytes 8388624 | tf_op jit(solution)/shard_map/all_gather | solution.py:80
  780.0 6.2 gather_fusion.2
  786.2 6.4 fusion.15
  (67 shorter events, 23.2 us)
Async XLA Ops:
  6.5 191.2 %reduce-scatter.4.cloned.1.call-start = ((), (), s32[]{:S(2)}) async-start(), calls=%async_computation.5 | async-start | bytes 4259840 | tf_op jit(solution)/shard_map/reduce_scatter | solution.py:55
  40.3 245.7 %all-gather.9.cloned.1.call-start = ((), (), s32[]{:S(2)}) async-start(), calls=%async_computation.4 | async-start | bytes 1064960 | tf_op jit(solution)/shard_map/all_gather | solution.py:67
  199.3 172.5 %all-reduce.3.cloned.1.call-start = ((), (), s32[]{:S(2)}) async-start(), calls=%async_computation.1 | async-start | bytes 2097152 | tf_op jit(solution)/shard_map/psum | solution.py:15
  289.5 317.0 %all-gather.5.cloned.1.call-start = ((), (), s32[]{:S(2)}) async-start(), calls=%async_computation.2 | async-start | bytes 1064960 | tf_op jit(solution)/shard_map/all_gather | solution.py:79
  460.1 57.4 %copy-start = (pred[4]{0:T(512)(128)(4,1)S(1)}, pred[4]{0:T(512)(128)(4,1)}, u32[]{:S(2)}) copy-start(pred[4]{0:T(512)(128)(4,1)} %get-tuple-element.21) | copy-start | bytes 16
  519.2 259.4 %all-gather.7.cloned.1.call-start = ((), (), s32[]{:S(2)}) async-start(), calls=%async_computation.3 | async-start | bytes 9437184 | tf_op jit(solution)/shard_map/all_gather | solution.py:80
Sparse Core Ops, SparseCore 0:
  40.5 157.2 reduce-scatter.3
  201.6 84.3 all-gather.8
  289.6 82.1 all-reduce.2
  519.3 87.1 all-gather.4
  609.0 169.5 all-gather.6
where the time goes:
time: 804 us; the launch traced here: 799 us
  waiting for transfers between devices  579 us (72%)
  other arithmetic  130 us (16%)
  local copies, waits for them, and re-layouts  55 us (7%)
  matrix products  18.6 us (2%)
  between operations  16.2 us (2%)
    all_gather x1, waiting for transfers between devices, body(): full_panel = lax.all_gather(by_rows, 'blk', axis=1, tiled=True)  170 us
    reduce_scatter x1, waiting for transfers between devices, body(): lax.psum_scatter(term.reshape(row_count * lax.axis_size('dp'), slot_count...  155 us
    all_gather x1, waiting for transfers between devices, body(): by_rows = lax.all_gather(panel_piece, 'dp', axis=0, tiled=True)  87.2 us
    all_gather x1, waiting for transfers between devices, body(): whole_slab = lax.all_gather(local_rows[:, 0, :], 'dp', axis=0, tiled=True)  86.6 us
    another operation x15, other arithmetic, body(): corner = jnp.linalg.cholesky(diag_block)  80.6 us
    psum x1, waiting for transfers between devices, from_root(): return lax.psum(kept, axis)  80.3 us
    another operation x3, other arithmetic, body(): lax.linalg.triangular_solve(corner, identity, left_side=True, lower=True)  41.9 us
  transfers between devices with their start and end apart: 5, of which 5 were waited for; matrix products, arithmetic and copies ran while one was open for 0% of the time, Pallas kernels for 0%

commit v1 on v0

v1 whole, which is shorter than its diff:
```python
import jax
import jax.numpy as jnp
import numpy as np
from jax import lax
from jax.experimental import pallas as pl
from jax.experimental.pallas import tpu as pltpu
from jax.sharding import PartitionSpec as P

BS = 512
HALF = 256
NB = 128
NZ, NY, NC, NBLK = 8, 4, 2, 8
TOKENS = 40960
DAMPING = 0.1
F32 = jnp.float32
VMEM_LIMIT = 40 * 1024 * 1024
GRAM_LIMIT = 60 * 1024 * 1024
CORNER_FLOPS = 20_000_000_000

HELD = (2, 1, 2, 3, 4, 5, 6, 1)
TRAIL = (
    ((6, 4), (2, 1), (5, 2)),
    ((5, 5), (6, 2), (3, 1)),
    ((3, 3), (6, 5), (4, 1)),
    ((6, 6), (5, 1), (4, 3)),
    ((6, 1), (5, 3), None),
    ((2, 2), None, (6, 3)),
    (None, (4, 4), (3, 2)),
    ((4, 2), (1, 1), (5, 4)),
)
ROUNDS = (
    ((3, 2), (4, 0), (5, 1), (6, 3), (7, 4), (2, 5), (0, 7)),
    ((3, 4), (4, 6), (5, 2), (1, 0), (7, 3), (0, 1)),
    ((3, 5), (4, 7), (1, 2), (2, 6)),
)


def owner_tables():
    count = BS * 7 // BS
    order = [(i, j) for j in range(count) for i in range(j, count)]
    slot_of = {pair: (t % NBLK, t // NBLK) for t, pair in enumerate(order)}
    rows = []
    for owner in range(NBLK):
        row = [HELD[owner], owner if 0 < owner < 7 else 1]
        for r in range(3):
            pair = TRAIL[owner][r]
            if pair is None:
                row += [1, 1, 0, 0, 0]
                continue
            at, slot = slot_of[pair]
            assert at == owner
            sent = [s for s, d in ROUNDS[r] if d == owner]
            own = 0 if sent else 1
            assert HELD[sent[0] if sent else owner] == pair[1]
            row += [pair[0], pair[1], 1, own, slot]
        rows.append(row)
    return np.asarray(rows, np.int32)


CORE, RANK, OWNER, HELD_AT, CORNER, ROW_I, COL_J, LIVE, OWN, SLOT, PANEL_SLOT = 0, 1, 2, 3, 4, 5, 9, 12, 15, 18, 21
WIDTH = 24


def device_table():
    per_owner = owner_tables()
    table = np.zeros((NZ * NY * NC * NBLK, WIDTH), np.int32)
    for group in range(NZ * NY * NC):
        for owner in range(NBLK):
            row = table[group * NBLK + owner]
            mine = per_owner[owner]
            row[CORE], row[RANK], row[OWNER] = group % NC, group // NC, owner
            row[HELD_AT], row[CORNER] = mine[0], owner == 0
            row[ROW_I] = mine[1]
            for e in range(3):
                i, j, live, own, slot = mine[2 + 5 * e : 7 + 5 * e]
                row[ROW_I + 1 + e], row[COL_J + e], row[LIVE + e], row[OWN + e], row[SLOT + e] = i, j, live, own, slot
            row[PANEL_SLOT] = 0 if owner < 7 else -1
    return table


def split(x):
    hi = x.astype(jnp.bfloat16)
    return hi, (x - hi.astype(F32)).astype(jnp.bfloat16)


def dot3(a, b, dims):
    def one(u, v):
        return lax.dot_general(u, v, (dims, ((), ())), preferred_element_type=F32)

    return one(a[0], b[0]) + (one(a[0], b[1]) + one(a[1], b[0]))


NT = ((1,), (1,))
NN = ((1,), (0,))
TN = ((0,), (0,))


def gram(a, b):
    return lax.dot_general(a, b, (TN, ((), ())), preferred_element_type=F32)


def first_column_kernel(s_ref, a0_ref, ai_ref, mine_ref, other_ref, d_ref):
    core = s_ref[CORE]
    owner = s_ref[OWNER]
    a0 = a0_ref[...]
    d_ref[...] = gram(a0, a0)
    for half in range(NC):
        block = gram(ai_ref[...], a0[:, half * HALF : (half + 1) * HALF])

        def store(out_ref):
            for z in range(NZ):
                row = pl.multiple_of(owner * 64 + z * 8, 8)
                out_ref[z, 0:8, :] = d_ref[pl.ds(row, 8), half * HALF : (half + 1) * HALF]
                out_ref[z, 8:72, :] = block[z * 64 : (z + 1) * 64, :]

        @pl.when(core == half)
        def _():
            store(mine_ref)

        @pl.when(core != half)
        def _():
            store(other_ref)


def sum_z_kernel(x_ref, after_ref, out_ref):
    del after_ref
    total = x_ref[0]
    for z in range(1, NZ):
        total = total + x_ref[z]
    for y in range(NY):
        out_ref[y] = total


def sum_y_kernel(s_ref, x_ref, after_ref, corner_ref, held_ref, rows_ref):
    del after_ref
    total = x_ref[0]
    for y in range(1, NY):
        total = total + x_ref[y]
    for z in range(NZ):
        corner_ref[z] = total[0:8, :]
        held_ref[z] = total[8:72, :]
    for y in range(NY):

        @pl.when(lax.rem(s_ref[RANK], NY) == y)
        def _():
            rows_ref[...] = total[8 + 16 * y : 24 + 16 * y, :]


HBM = pl.BlockSpec(memory_space=pltpu.HBM)


def trailing_kernel(s_ref, ai_ref, aj_ref, after_ref, mine_ref, other_ref):
    del after_ref
    core = s_ref[CORE]
    block = gram(ai_ref[...], aj_ref[...])
    for half in range(NC):

        def store(out_ref):
            for q in range(NZ * NY):
                out_ref[8 * q : 8 * q + 8, :] = block[16 * q + 8 * half : 16 * q + 8 * half + 8, :]

        @pl.when(core == half)
        def _():
            store(mine_ref)

        @pl.when(core != half)
        def _():
            store(other_ref)


def eliminate(T):
    n = len(T)
    T = list(T)
    lane = lax.broadcasted_iota(jnp.int32, (8, NB), 1)
    sub = lax.broadcasted_iota(jnp.int32, (8, NB), 0)
    out = [None] * n
    for g in range(n):
        c0 = 8 * g
        V = [jnp.broadcast_to(T[g][:, c0 + k : c0 + k + 1], (8, NB)) for k in range(8)]
        ingroup = (lane >= c0) & (lane < c0 + 8)
        R = jnp.where(ingroup, jnp.where(lane == sub + c0, 1.0, 0.0), T[g])
        rcp, d, rows = [], [], []
        pivot = jnp.ones((8, NB), F32)
        for k in range(8):
            dk = [jnp.broadcast_to(V[j][k : k + 1, :], (8, NB)) for j in range(k, 8)]
            r = 1.0 / dk[0]
            pivot = jnp.where(sub == k, dk[0], pivot)
            Rk = jnp.broadcast_to(R[k : k + 1, :], (8, NB))
            rcp.append(r)
            d.append(dk)
            rows.append(Rk)
            if k < 7:
                m = jnp.where(sub > k, V[k] * r, 0.0)
                for j in range(k + 1, 8):
                    V[j] = V[j] - m * dk[j - k]
                R = R - m * Rk
        out[g] = jnp.where(lane < c0 + 8, R * lax.rsqrt(pivot), 0.0)
        for s in range(g + 1, n):
            V = [jnp.broadcast_to(T[s][:, c0 + k : c0 + k + 1], (8, NB)) for k in range(8)]
            R = jnp.where(ingroup, 0.0, T[s])
            for k in range(8):
                m = V[k] * rcp[k]
                for j in range(k + 1, 8):
                    V[j] = V[j] - m * d[k][j - k]
                R = R - m * rows[k]
            T[s] = R
    return out


def corner_kernel(s_ref, mine_ref, other_ref, p_ref, w_ref, a_ref, c_ref, i_ref, x_ref, px_ref):
    core = s_ref[CORE]
    rank = s_ref[RANK]
    is_corner = s_ref[CORNER]
    n = BS // NB
    scale = 1.0 / TOKENS
    for half in range(NC):
        cols = slice(half * HALF, (half + 1) * HALF)

        def load(src_ref):
            for o in range(NBLK):
                a_ref[64 * o : 64 * o + 64, cols] = src_ref[o, 0:64, :] * scale
            for q in range(4):
                x_ref[16 * q : 16 * q + 16, cols] = src_ref[s_ref[ROW_I + q], 64:80, :] * scale

        @pl.when(core == half)
        def _():
            load(mine_ref)

        @pl.when(core != half)
        def _():
            load(other_ref)

    row = lax.broadcasted_iota(jnp.int32, (NB, NB), 0)
    col = lax.broadcasted_iota(jnp.int32, (NB, NB), 1)
    for b in range(n):
        at = slice(b * NB, (b + 1) * NB)
        a_ref[at, at] = a_ref[at, at] + jnp.where(row == col, DAMPING, 0.0)

    @pl.when(is_corner == 1)
    def _():
        x_ref[0:16, :] = a_ref[pl.ds(pl.multiple_of(rank * 16, 16), 16), :]

    for b in range(n):
        o = b * NB
        out = eliminate([a_ref[o + 8 * g : o + 8 * g + 8, o : o + NB] for g in range(NB // 8)])
        for g in range(NB // 8):
            i_ref[b, 8 * g : 8 * g + 8, :] = out[g]
        inv = split(i_ref[b])
        xf = dot3(split(x_ref[:, o : o + NB]), inv, NT)
        px_ref[:, o : o + NB] = xf
        if b < n - 1:
            X = dot3(split(a_ref[o + NB :, o : o + NB]), inv, NT)
            c_ref[o + NB :, o : o + NB] = X
            Xs = split(X)
            a_ref[o + NB :, o + NB :] = a_ref[o + NB :, o + NB :] - dot3(Xs, Xs, NT)
            x_ref[:, o + NB :] = x_ref[:, o + NB :] - dot3(split(xf), Xs, NT)
    panel = px_ref[0:16, :]
    grow = rank * 16 + lax.broadcasted_iota(jnp.int32, (16, BS), 0)
    gcol = lax.broadcasted_iota(jnp.int32, (16, BS), 1)
    panel = jnp.where((is_corner == 1) & (gcol > grow), 0.0, panel)
    p_ref[...] = panel
    ws = [None] * n
    wv = [None] * n
    for b in reversed(range(n)):
        o = b * NB
        acc = px_ref[16:, o : o + NB]
        for i in range(b + 1, n):
            acc = acc - dot3(ws[i], split(c_ref[i * NB : (i + 1) * NB, o : o + NB]), NN)
        wv[b] = dot3(split(acc), split(i_ref[b]), NN)
        ws[b] = split(wv[b])
    for half in range(NC):

        @pl.when(core == half)
        def _():
            for q in range(2):
                w_ref[:, q * NB : (q + 1) * NB] = wv[2 * half + q]


def update_kernel(s_ref, w_ref, own_ref, r0_ref, r1_ref, r2_ref, mine_ref, other_ref):
    core = s_ref[CORE]
    for e, recv_ref in enumerate((r0_ref, r1_ref, r2_ref)):
        own = s_ref[OWN + e]
        got = jnp.where(own == 1, own_ref[...], recv_ref[...])
        part = dot3(split(w_ref[16 * e : 16 * e + 16, :]), split(got), NT)
        cols = slice(e * BS, (e + 1) * BS)
        low, high = part[0:8, :], part[8:16, :]
        mine_ref[:, cols] = jnp.where(core == 0, low, high)
        other_ref[:, cols] = jnp.where(core == 0, high, low)


def finish_kernel(s_ref, panel_ref, rest_ref, mine_ref, other_ref, out_ref):
    core = s_ref[CORE]
    row = s_ref[RANK] * 16 + core * 8 + lax.broadcasted_iota(jnp.int32, (8, BS), 0)
    col = lax.broadcasted_iota(jnp.int32, (8, BS), 1)
    panel = jnp.where(core == 0, panel_ref[0:8, :], panel_ref[8:16, :])
    values = []
    for e in range(3):
        cols = slice(e * BS, (e + 1) * BS)
        value = (rest_ref[:, cols] - (mine_ref[:, cols] + other_ref[:, cols])) * (1.0 / TOKENS)
        on_diagonal = s_ref[ROW_I + 1 + e] == s_ref[COL_J + e]
        values.append(value + jnp.where(on_diagonal & (row == col), DAMPING, 0.0))
    for slot in range(4):
        out = jnp.where(s_ref[PANEL_SLOT] == slot, panel, 0.0)
        for e in range(3):
            out = jnp.where((s_ref[SLOT + e] == slot) & (s_ref[LIVE + e] == 1), values[e], out)
        out_ref[:, slot * BS : (slot + 1) * BS] = out


def vmem(count):
    return [pl.BlockSpec(memory_space=pltpu.VMEM)] * count


SMEM = pl.BlockSpec(memory_space=pltpu.SMEM)


def params(limit=VMEM_LIMIT):
    return pltpu.CompilerParams(vmem_limit_bytes=limit)


def dp_index(z, y, c):
    return (z * NY + y) * NC + c


Z_GROUPS = [[dp_index(z, y, c) for z in range(NZ)] for y in range(NY) for c in range(NC)]
Y_GROUPS = [[dp_index(z, y, c) for y in range(NY)] for z in range(NZ) for c in range(NC)]
CORE_SWAP = [(dp_index(z, y, c), dp_index(z, y, 1 - c)) for z in range(NZ) for y in range(NY) for c in range(NC)]


def exchange(x, groups):
    return lax.all_to_all(x, "dp", 0, 0, axis_index_groups=groups)


def body(act):
    tok = act.shape[0]
    group = lax.axis_index("dp")
    place = lax.dynamic_index_in_dim(
        jnp.asarray(device_table()), group * NBLK + lax.axis_index("blk"), 0, keepdims=False
    )

    piece = jax.ShapeDtypeStruct((NZ, 72, HALF), F32)
    mine, other = pl.pallas_call(
        first_column_kernel,
        out_shape=[piece, piece],
        grid_spec=pltpu.PrefetchScalarGridSpec(
            num_scalar_prefetch=1,
            grid=(1,),
            in_specs=[
                pl.BlockSpec((tok, BS), lambda g, s: (0, 0)),
                pl.BlockSpec((tok, BS), lambda g, s: (0, s[HELD_AT])),
            ],
            out_specs=[pl.BlockSpec((NZ, 72, HALF), lambda g, s: (0, 0, 0))] * 2,
            scratch_shapes=[pltpu.VMEM((BS, BS), F32)],
        ),
        compiler_params=params(GRAM_LIMIT),
        name="first_column",
    )(place, act, act)
    first = mine + lax.ppermute(other, "dp", CORE_SWAP)
    over_z = exchange(first, Z_GROUPS)

    wide = jax.ShapeDtypeStruct((BS // 2, 3 * BS), F32)
    mine, other = pl.pallas_call(
        trailing_kernel,
        out_shape=[wide, wide],
        grid_spec=pltpu.PrefetchScalarGridSpec(
            num_scalar_prefetch=1,
            grid=(3,),
            in_specs=[
                pl.BlockSpec((tok, BS), lambda e, s: (0, s[ROW_I + 1 + e])),
                pl.BlockSpec((tok, BS), lambda e, s: (0, s[COL_J + e])),
                HBM,
            ],
            out_specs=[pl.BlockSpec((BS // 2, BS), lambda e, s: (0, e))] * 2,
        ),
        compiler_params=params(GRAM_LIMIT),
        cost_estimate=pl.CostEstimate(flops=4_000_000_000, bytes_accessed=7_000_000, transcendentals=0),
        name="trailing_gram",
    )(place, act, act, first)
    both = mine + lax.ppermute(other, "dp", CORE_SWAP)
    rest = lax.psum_scatter(both, "dp", scatter_dimension=0, tiled=True, axis_index_groups=Z_GROUPS)
    rest = lax.psum_scatter(rest, "dp", scatter_dimension=0, tiled=True, axis_index_groups=Y_GROUPS)

    spread = pl.pallas_call(
        sum_z_kernel,
        out_shape=jax.ShapeDtypeStruct((NY, 72, HALF), F32),
        in_specs=vmem(1) + [HBM],
        out_specs=vmem(1)[0],
        name="sum_over_z",
    )(over_z, other)
    over_y = exchange(spread, Y_GROUPS)
    corner_rows, held_rows, own_rows = pl.pallas_call(
        sum_y_kernel,
        out_shape=[
            jax.ShapeDtypeStruct((NZ, 8, HALF), F32),
            jax.ShapeDtypeStruct((NZ, 64, HALF), F32),
            jax.ShapeDtypeStruct((16, HALF), F32),
        ],
        in_specs=[SMEM] + vmem(1) + [HBM],
        out_specs=vmem(3),
        name="sum_over_y",
    )(place, over_y, both)

    corner_rows = exchange(corner_rows, Z_GROUPS)
    column = exchange(held_rows, Z_GROUPS).reshape(BS, HALF)
    share = jnp.concatenate([corner_rows.reshape(64, HALF), own_rows], axis=0)
    share = lax.all_to_all(jnp.broadcast_to(share, (NBLK, 80, HALF)), "blk", 0, 0)
    share_other = lax.ppermute(share, "dp", CORE_SWAP)
    brought = [lax.ppermute(column, "blk", list(pairs)) for pairs in ROUNDS]

    panel, w = pl.pallas_call(
        corner_kernel,
        out_shape=[jax.ShapeDtypeStruct((16, BS), F32), jax.ShapeDtypeStruct((48, HALF), F32)],
        in_specs=[SMEM] + vmem(2),
        out_specs=vmem(2),
        scratch_shapes=[
            pltpu.VMEM((BS, BS), F32),
            pltpu.VMEM((BS, BS), F32),
            pltpu.VMEM((BS // NB, NB, NB), F32),
            pltpu.VMEM((64, BS), F32),
            pltpu.VMEM((64, BS), F32),
        ],
        compiler_params=params(),
        cost_estimate=pl.CostEstimate(flops=CORNER_FLOPS, bytes_accessed=2_000_000, transcendentals=0),
        name="corner",
    )(place, share, share_other)

    part = jax.ShapeDtypeStruct((8, 3 * BS), F32)
    mine, other = pl.pallas_call(
        update_kernel,
        out_shape=[part, part],
        in_specs=[SMEM] + vmem(5),
        out_specs=vmem(2),
        compiler_params=params(),
        name="update",
    )(place, w, column, *brought)
    return pl.pallas_call(
        finish_kernel,
        out_shape=jax.ShapeDtypeStruct((8, 4 * BS), F32),
        in_specs=[SMEM] + vmem(4),
        out_specs=vmem(1)[0],
        name="finish",
    )(place, panel, rest, mine, lax.ppermute(other, "dp", CORE_SWAP))


def solution(mesh):
    return jax.shard_map(body, mesh=mesh, in_specs=(P("dp", None),), out_specs=P("dp", "blk"), check_vma=False)
```

time: 804 us -> 170 us (0.21)
  waiting for transfers between devices: 579 us -> 23.9 us
  other arithmetic: 130 us -> 5.46 us
  local copies, waits for them, and re-layouts: 55 us -> 3.38 us
  starting transfers between devices: 0.63 us -> 44.9 us
  blocking collectives: 0 us -> 39.9 us
  Pallas kernels: 0 us -> 37.6 us
  matrix products: 18.6 us -> 0 us
    all_gather x3 -> x0, waiting for transfers between devices: 344 us -> none  [the longest x1 170 us: body(): full_panel = lax.all_gather(by_rows, 'blk', axis=1, tiled=True)]
    reduce_scatter x1 -> x2, waiting for transfers between devices: 155 us -> 0.02 us  [the longest x1 0.02 us: body(): lax.psum_scatter(both, 'dp', scatter_dimension=0, tiled=True, axis_index_...]
    another operation x18 -> x0, other arithmetic: 123 us -> none  [the longest x15 80.6 us: body(): corner = jnp.linalg.cholesky(diag_block)]
    psum x1 -> x0, waiting for transfers between devices: 80.3 us -> none  [from_root(): return lax.psum(kept, axis)]
    all_to_all x0 -> x3, blocking collectives: none -> 39.9 us  [the longest x2 27.5 us: exchange(): return lax.all_to_all(x, 'dp', 0, 0, axis_index_groups=groups)]
    pallas_call x0 -> x7, Pallas kernels: none -> 37.6 us  [the longest x1 20.2 us: body(): pl.pallas_call(corner_kernel, out_shape=[jax.ShapeDtypeStruct((16, BS), F...]
    ppermute x0 -> x7, starting transfers between devices: none -> 36.6 us  [the longest x1 9.41 us: body(): lax.ppermute(other, 'dp', CORE_SWAP)]
    all_to_all x0 -> x2, waiting for transfers between devices: none -> 21.1 us  [exchange(): return lax.all_to_all(x, 'dp', 0, 0, axis_index_groups=groups)]
  transfers between devices with their start and end apart: 5 -> 11, of which waited for: 5 -> 4; matrix products, arithmetic and copies ran while one was open for 0% -> 2% of each run, Pallas kernels for 0% -> 15%
where the time goes in v1:
time: 170 us; the launch traced here: 169 us
  starting transfers between devices  44.9 us (26%)
  blocking collectives  39.9 us (23%)
  Pallas kernels  37.6 us (22%)
  waiting for transfers between devices  23.9 us (14%)
  between operations  13.6 us (8%)
  other arithmetic  5.46 us (3%)
  local copies, waits for them, and re-layouts  3.38 us (2%)
    all_to_all x2, blocking collectives, exchange(): return lax.all_to_all(x, 'dp', 0, 0, axis_index_groups=groups)  27.5 us
    all_to_all x2, waiting for transfers between devices, exchange(): return lax.all_to_all(x, 'dp', 0, 0, axis_index_groups=groups)  21.1 us
    pallas_call x1, Pallas kernels, body(): pl.pallas_call(corner_kernel, out_shape=[jax.ShapeDtypeStruct((16, BS), F...  20.2 us
    all_to_all x1, blocking collectives, body(): lax.all_to_all(jnp.broadcast_to(share, (NBLK, 80, HALF)), 'blk', 0, 0)  12.4 us
    ppermute x1, starting transfers between devices, body(): lax.ppermute(other, 'dp', CORE_SWAP)  9.41 us
    ppermute x1, starting transfers between devices, body(): first = mine + lax.ppermute(other, 'dp', CORE_SWAP)  8.77 us
    ppermute x3, starting transfers between devices, body(): brought = [lax.ppermute(column, 'blk', list(pairs)) for pairs in ROUNDS]  8.56 us
    all_to_all x2, starting transfers between devices, exchange(): return lax.all_to_all(x, 'dp', 0, 0, axis_index_groups=groups)  8.16 us
  transfers between devices with their start and end apart: 11, of which 4 were waited for; matrix products, arithmetic and copies ran while one was open for 2% of the time, Pallas kernels for 15%

profile of v1, /device:TPU:1, one launch (start us, length us, event | category | flops | bytes accessed | tf_op | source)
XLA Modules:
  0.0 168.6 jit_solution(5643060577076906566)
XLA Ops:
  6.5 1.3 dynamic-slice_bitcast_fusion.s_ref
  7.8 4.6 %first_column.1 = (f32[8,72,256]{2,1,0:T(8,128)}, f32[8,72,256]{2,1,0:T(8,128)}) custom-call(s32[24]{0:T(128)} %dynamic-slice_bitcast_fusion.s_ref, bf16[640,3584]{1,0:T(8,128)(2,1)} %aj_ref.1, bf16[640,3584]{1,0:T(8,128)(2,1)} %aj_ref.1), custom_call_target="tpu_custom_call" | custom-call | tf_op jit(solution)/shard_map/first_column/pallas_call | solution.py:341
  12.5 8.8 %collective-permute-start = (f32[8,72,256]{2,1,0:T(8,128)}, f32[8,72,256]{2,1,0:T(8,128)S(1)}, u32[]{:S(2)}, u32[]{:S(2)}) collective-permute-start(f32[8,72,256]{2,1,0:T(8,128)} %get-tuple-element.17), channel_id=1, source_target_pairs={{0,8},{8,0},{16,24},{24,16},{32,40},{40,32},{48,56},{56,48},{64,72... | collective-permute-start | bytes 1769480 | tf_op jit(solution)/shard_map/ppermute | solution.py:357
  21.2 1.8 %collective-permute-done = f32[8,72,256]{2,1,0:T(8,128)S(1)} collective-permute-done((f32[8,72,256]{2,1,0:T(8,128)}, f32[8,72,256]{2,1,0:T(8,128)S(1)}, u32[]{:S(2)}, u32[]{:S(2)}) %collective-permute-start) | collective-permute-done | bytes 589856 | tf_op jit(solution)/shard_map/ppermute | solution.py:357
  23.1 2.0 %add.19.after_ref = f32[8,72,256]{2,1,0:T(8,128)} add(f32[8,72,256]{2,1,0:T(8,128)} %get-tuple-element.16, f32[8,72,256]{2,1,0:T(8,128)S(1)} %collective-permute-done) | non-fusion elementwise | flops 147456 | bytes 1769472 | tf_op jit(solution)/shard_map/add | solution.py:357
  25.0 6.2 %trailing_gram.1 = (f32[256,1536]{1,0:T(8,128)}, f32[256,1536]{1,0:T(8,128)}) custom-call(s32[24]{0:T(128)} %dynamic-slice_bitcast_fusion.s_ref, bf16[640,3584]{1,0:T(8,128)(2,1)} %aj_ref.1, bf16[640,3584]{1,0:T(8,128)(2,1)} %aj_ref.1, f32[8,72,256]{2,1,0:T(8,128)} %add.19.after_ref), custom_call_target="tpu_custom_call" | custom-call | flops 4000000000 | bytes 7000000 | tf_op jit(solution)/shard_map/trailing_gram/pallas_call | solution.py:361
  31.2 2.3 %collective-permute-start.1 = (f32[256,1536]{1,0:T(8,128)}, f32[256,1536]{1,0:T(8,128)S(1)}, u32[]{:S(2)}, u32[]{:S(2)}) collective-permute-start(f32[256,1536]{1,0:T(8,128)} %get-tuple-element.18.after_ref), channel_id=1, source_target_pairs={{0,8},{8,0},{16,24},{24,16},{32,40},{40,32},{48,56},{56,48},{64,72... | collective-permute-start | bytes 4718600 | tf_op jit(solution)/shard_map/ppermute | solution.py:378
  33.5 4.7 %all-to-all-start = ((f32[8,72,256]{2,1,0:T(8,128)}), f32[8,72,256]{2,1,0:T(8,128)S(1)}, u32[]{:S(2)}, u32[]{:S(2)}) async-start(f32[8,72,256]{2,1,0:T(8,128)} %add.19.after_ref), calls=%async_computation | async-start | bytes 1179648 | tf_op jit(solution)/shard_map/all_to_all | solution.py:330
  38.2 0.0 reduce-scatter.3.cloned.1.call-start
  38.2 2.8 %add.20.after_ref = f32[256,1536]{1,0:T(8,128)} add(f32[256,1536]{1,0:T(8,128)} %get-tuple-element.19, f32[256,1536]{1,0:T(8,128)S(1)} %collective-permute-done.1) | non-fusion elementwise | flops 393216 | bytes 4718592 | tf_op jit(solution)/shard_map/add | solution.py:378
  41.0 16.6 %all-to-all-done.x_ref = f32[8,72,256]{2,1,0:T(8,128)S(1)} async-done(((f32[8,72,256]{2,1,0:T(8,128)}), f32[8,72,256]{2,1,0:T(8,128)S(1)}, u32[]{:S(2)}, u32[]{:S(2)}) %all-to-all-start) | async-done | bytes 589856 | tf_op jit(solution)/shard_map/all_to_all | solution.py:330
  57.6 0.8 copy-done.3
  58.4 1.8 %sum_over_z.1 = f32[4,72,256]{2,1,0:T(8,128)} custom-call(f32[8,72,256]{2,1,0:T(8,128)} %copy-done.3, f32[256,1536]{1,0:T(8,128)} %get-tuple-element.18.after_ref), custom_call_target="tpu_custom_call" | custom-call | tf_op jit(solution)/shard_map/sum_over_z/pallas_call | solution.py:382
  60.2 17.0 %all_to_all.25.x_ref = f32[4,72,256]{2,1,0:T(8,128)} all-to-all(f32[4,72,256]{2,1,0:T(8,128)} %sum_over_z.1), channel_id=1, replica_groups={{0,16,32,48},{8,24,40,56},{64,80,96,112},{72,88,104,120},{128,144,160,1..., dimensions={0} | all-to-all | bytes 589824 | tf_op jit(solution)/shard_map/all_to_all | solution.py:330
  77.2 1.9 %sum_over_y.1 = (f32[8,8,256]{2,1,0:T(8,128)}, f32[8,64,256]{2,1,0:T(8,128)}, f32[16,256]{1,0:T(8,128)}) custom-call(s32[24]{0:T(128)} %dynamic-slice_bitcast_fusion.s_ref, f32[4,72,256]{2,1,0:T(8,128)} %all_to_all.25.x_ref, f32[256,1536]{1,0:T(8,128)} %add.20.after_ref), custom_call_target="tpu_custom_call" | custom-call | tf_op jit(solution)/shard_map/sum_over_y/pallas_call | solution.py:390
  79.1 10.5 %all_to_all.26 = f32[8,8,256]{2,1,0:T(8,128)S(1)} all-to-all(f32[8,8,256]{2,1,0:T(8,128)} %get-tuple-element.20), channel_id=1, replica_groups={{0,64,128,192,256,320,384,448},{8,72,136,200,264,328,392,456},{16,80,14..., dimensions={0} | all-to-all | bytes 131072 | tf_op jit(solution)/shard_map/all_to_all | solution.py:330
  89.6 0.7 pad_maximum_fusion
  90.4 12.4 %all_to_all.27.mine_ref = f32[8,80,256]{2,1,0:T(8,128)S(1)} all-to-all(f32[8,80,256]{2,1,0:T(8,128)S(1)} %broadcast_in_dim.3), channel_id=1, replica_groups=mesh['dp'=64,'blk'=8] {'blk'}, dimensions={0} | all-to-all | bytes 1310720 | tf_op jit(solution)/shard_map/all_to_all | solution.py:405
  102.7 3.5 %all-to-all-start.4 = ((f32[8,64,256]{2,1,0:T(8,128)}), f32[8,64,256]{2,1,0:T(8,128)S(1)}, u32[]{:S(2)}, u32[]{:S(2)}) async-start(f32[8,64,256]{2,1,0:T(8,128)} %get-tuple-element.24), calls=%async_computation.6 | async-start | bytes 1048576 | tf_op jit(solution)/shard_map/all_to_all | solution.py:330
  106.2 0.0 reduce-scatter.5.cloned.1.call-start
  106.3 7.6 %collective-permute-start.2 = (f32[8,80,256]{2,1,0:T(8,128)S(1)}, f32[8,80,256]{2,1,0:T(8,128)S(1)}, u32[]{:S(2)}, u32[]{:S(2)}) collective-permute-start(f32[8,80,256]{2,1,0:T(8,128)S(1)} %all_to_all.27.mine_ref), channel_id=1, source_target_pairs={{0,8},{8,0},{16,24},{24,16},{32,40},{40,32},{48,56},{56,48},{64,72... | collective-permute-start | bytes 1966088 | tf_op jit(solution)/shard_map/ppermute | solution.py:406
  113.9 4.5 %all-to-all-done.4 = f32[8,64,256]{2,1,0:T(8,128)S(1)} async-done(((f32[8,64,256]{2,1,0:T(8,128)}), f32[8,64,256]{2,1,0:T(8,128)S(1)}, u32[]{:S(2)}, u32[]{:S(2)}) %all-to-all-start.4) | async-done | bytes 524320 | tf_op jit(solution)/shard_map/all_to_all | solution.py:330
  118.5 0.7 collective-permute-start.5
  119.2 4.4 %collective-permute-start.4 = (f32[512,256]{1,0:T(8,128)S(1)}, f32[512,256]{1,0:T(8,128)S(1)}, u32[]{:S(2)}, u32[]{:S(2)}) collective-permute-start(f32[512,256]{1,0:T(8,128)S(1)} %bitcast.5), channel_id=1, source_target_pairs={{3,4},{4,6},{5,2},{1,0},{7,3},{0,1},{11,12},{12,14},{13,10},{9,8},... | collective-permute-start | bytes 1572872 | tf_op jit(solution)/shard_map/ppermute | solution.py:407
  123.6 3.4 %collective-permute-start.3 = (f32[512,256]{1,0:T(8,128)S(1)}, f32[512,256]{1,0:T(8,128)S(1)}, u32[]{:S(2)}, u32[]{:S(2)}) collective-permute-start(f32[512,256]{1,0:T(8,128)S(1)} %bitcast.6), channel_id=1, source_target_pairs={{3,2},{4,0},{5,1},{6,3},{7,4},{2,5},{0,7},{11,10},{12,8},{13,9},{1... | collective-permute-start | bytes 1572872 | tf_op jit(solution)/shard_map/ppermute | solution.py:407
  127.1 20.2 %corner.1 = (f32[16,512]{1,0:T(8,128)S(1)}, f32[48,256]{1,0:T(8,128)S(1)}) custom-call(s32[24]{0:T(128)S(1)} %copy-done.2, f32[8,80,256]{2,1,0:T(8,128)S(1)} %all_to_all.27.mine_ref, f32[8,80,256]{2,1,0:T(8,128)S(1)} %collective-permute-done.2.other_ref), custom_call_target="tpu_custom_call" | custom-call | flops 20000000000 | bytes 2000000 | tf_op jit(solution)/shard_map/corner/pallas_call | solution.py:409
  147.4 1.3 update.1
  148.7 0.6 copy-done
  149.3 9.4 %collective-permute-start.6 = (f32[8,1536]{1,0:T(8,128)S(1)}, f32[8,1536]{1,0:T(8,128)S(1)}, u32[]{:S(2)}, u32[]{:S(2)}) collective-permute-start(f32[8,1536]{1,0:T(8,128)S(1)} %get-tuple-element.26), channel_id=1, source_target_pairs={{0,8},{8,0},{16,24},{24,16},{32,40},{40,32},{48,56},{56,48},{64,72... | collective-permute-start | bytes 147464 | tf_op jit(solution)/shard_map/ppermute | solution.py:441
  158.7 0.9 collective-permute-done.6.other_ref
  159.6 0.6 copy-done.4
  160.2 1.5 finish.1
  (17 shorter events, 0.1 us)
Async XLA Ops:
  12.5 10.6 %collective-permute-start = (f32[8,72,256]{2,1,0:T(8,128)}, f32[8,72,256]{2,1,0:T(8,128)S(1)}, u32[]{:S(2)}, u32[]{:S(2)}) collective-permute-start(f32[8,72,256]{2,1,0:T(8,128)} %get-tuple-element.17), channel_id=1, source_target_pairs={{0,8},{8,0},{16,24},{24,16},{32,40},{40,32},{48,56},{56,48},{64,72... | collective-permute-start | bytes 1769480 | tf_op jit(solution)/shard_map/ppermute | solution.py:357
  31.2 7.0 %collective-permute-start.1 = (f32[256,1536]{1,0:T(8,128)}, f32[256,1536]{1,0:T(8,128)S(1)}, u32[]{:S(2)}, u32[]{:S(2)}) collective-permute-start(f32[256,1536]{1,0:T(8,128)} %get-tuple-element.18.after_ref), channel_id=1, source_target_pairs={{0,8},{8,0},{16,24},{24,16},{32,40},{40,32},{48,56},{56,48},{64,72... | collective-permute-start | bytes 4718600 | tf_op jit(solution)/shard_map/ppermute | solution.py:378
  33.5 24.1 %all-to-all-start = ((f32[8,72,256]{2,1,0:T(8,128)}), f32[8,72,256]{2,1,0:T(8,128)S(1)}, u32[]{:S(2)}, u32[]{:S(2)}) async-start(f32[8,72,256]{2,1,0:T(8,128)} %add.19.after_ref), calls=%async_computation | async-start | bytes 1179648 | tf_op jit(solution)/shard_map/all_to_all | solution.py:330
  38.2 88.9 %reduce-scatter.3.cloned.1.call-start = ((), (), s32[]{:S(2)}) async-start(), calls=%async_computation.7 | async-start | bytes 1769472 | tf_op jit(solution)/shard_map/reduce_scatter | solution.py:379
  57.6 0.8 copy-start.3
  90.3 36.8 %copy-start.2 = (s32[24]{0:T(128)S(1)}, s32[24]{0:T(128)}, u32[]{:S(2)}) copy-start(s32[24]{0:T(128)} %dynamic-slice_bitcast_fusion.s_ref) | copy-start | bytes 292
  102.7 15.7 %all-to-all-start.4 = ((f32[8,64,256]{2,1,0:T(8,128)}), f32[8,64,256]{2,1,0:T(8,128)S(1)}, u32[]{:S(2)}, u32[]{:S(2)}) async-start(f32[8,64,256]{2,1,0:T(8,128)} %get-tuple-element.24), calls=%async_computation.6 | async-start | bytes 1048576 | tf_op jit(solution)/shard_map/all_to_all | solution.py:330
  106.2 53.4 %reduce-scatter.5.cloned.1.call-start = ((), (), s32[]{:S(2)}) async-start(), calls=%async_computation.8 | async-start | bytes 245760 | tf_op jit(solution)/shard_map/reduce_scatter | solution.py:380
  106.3 20.8 %collective-permute-start.2 = (f32[8,80,256]{2,1,0:T(8,128)S(1)}, f32[8,80,256]{2,1,0:T(8,128)S(1)}, u32[]{:S(2)}, u32[]{:S(2)}) collective-permute-start(f32[8,80,256]{2,1,0:T(8,128)S(1)} %all_to_all.27.mine_ref), channel_id=1, source_target_pairs={{0,8},{8,0},{16,24},{24,16},{32,40},{40,32},{48,56},{56,48},{64,72... | collective-permute-start | bytes 1966088 | tf_op jit(solution)/shard_map/ppermute | solution.py:406
  118.5 28.9 %collective-permute-start.5 = (f32[512,256]{1,0:T(8,128)S(1)}, f32[512,256]{1,0:T(8,128)S(1)}, u32[]{:S(2)}, u32[]{:S(2)}) collective-permute-start(f32[512,256]{1,0:T(8,128)S(1)} %bitcast.4), channel_id=1, source_target_pairs={{3,5},{4,7},{1,2},{2,6},{11,13},{12,15},{9,10},{10,14},{19,21},{20... | collective-permute-start | bytes 1572872 | tf_op jit(solution)/shard_map/ppermute | solution.py:407
  119.2 28.2 %collective-permute-start.4 = (f32[512,256]{1,0:T(8,128)S(1)}, f32[512,256]{1,0:T(8,128)S(1)}, u32[]{:S(2)}, u32[]{:S(2)}) collective-permute-start(f32[512,256]{1,0:T(8,128)S(1)} %bitcast.5), channel_id=1, source_target_pairs={{3,4},{4,6},{5,2},{1,0},{7,3},{0,1},{11,12},{12,14},{13,10},{9,8},... | collective-permute-start | bytes 1572872 | tf_op jit(solution)/shard_map/ppermute | solution.py:407
  123.6 23.8 %collective-permute-start.3 = (f32[512,256]{1,0:T(8,128)S(1)}, f32[512,256]{1,0:T(8,128)S(1)}, u32[]{:S(2)}, u32[]{:S(2)}) collective-permute-start(f32[512,256]{1,0:T(8,128)S(1)} %bitcast.6), channel_id=1, source_target_pairs={{3,2},{4,0},{5,1},{6,3},{7,4},{2,5},{0,7},{11,10},{12,8},{13,9},{1... | collective-permute-start | bytes 1572872 | tf_op jit(solution)/shard_map/ppermute | solution.py:407
  147.4 1.3 copy-start.1
  148.7 0.6 copy-start
  149.3 10.3 %collective-permute-start.6 = (f32[8,1536]{1,0:T(8,128)S(1)}, f32[8,1536]{1,0:T(8,128)S(1)}, u32[]{:S(2)}, u32[]{:S(2)}) collective-permute-start(f32[8,1536]{1,0:T(8,128)S(1)} %get-tuple-element.26), channel_id=1, source_target_pairs={{0,8},{8,0},{16,24},{24,16},{32,40},{40,32},{48,56},{56,48},{64,72... | collective-permute-start | bytes 147464 | tf_op jit(solution)/shard_map/ppermute | solution.py:441
  159.6 0.6 copy-start.4
Sparse Core Ops, SparseCore 0:
  41.9 41.1 reduce-scatter.2
  127.2 26.5 reduce-scatter.4

commit v2 on v1

--- a/solution.py
+++ b/solution.py
@@ -122,8 +122,7 @@
             store(other_ref)
 
 
-def sum_z_kernel(x_ref, after_ref, out_ref):
-    del after_ref
+def sum_z_kernel(x_ref, out_ref):
     total = x_ref[0]
     for z in range(1, NZ):
         total = total + x_ref[z]
@@ -131,8 +130,7 @@
         out_ref[y] = total
 
 
-def sum_y_kernel(s_ref, x_ref, after_ref, corner_ref, held_ref, rows_ref):
-    del after_ref
+def sum_y_kernel(s_ref, x_ref, corner_ref, held_ref, rows_ref):
     total = x_ref[0]
     for y in range(1, NY):
         total = total + x_ref[y]
@@ -146,26 +144,40 @@
             rows_ref[...] = total[8 + 16 * y : 24 + 16 * y, :]
 
 
+def pass_kernel(x_ref, after_ref, out_ref):
+    del x_ref, after_ref, out_ref
+
+
 HBM = pl.BlockSpec(memory_space=pltpu.HBM)
 
 
-def trailing_kernel(s_ref, ai_ref, aj_ref, after_ref, mine_ref, other_ref):
-    del after_ref
-    core = s_ref[CORE]
-    block = gram(ai_ref[...], aj_ref[...])
-    for half in range(NC):
-
-        def store(out_ref):
-            for q in range(NZ * NY):
-                out_ref[8 * q : 8 * q + 8, :] = block[16 * q + 8 * half : 16 * q + 8 * half + 8, :]
-
-        @pl.when(core == half)
-        def _():
-            store(mine_ref)
-
-        @pl.when(core != half)
-        def _():
-            store(other_ref)
+def after(x, dep):
+    return pl.pallas_call(
+        pass_kernel,
+        out_shape=jax.ShapeDtypeStruct(x.shape, x.dtype),
+        in_specs=[HBM, HBM],
+        out_specs=HBM,
+        input_output_aliases={0: 0},
+        name="after",
+    )(x, dep)
+
+
+def trailing_kernel(s_ref, ai_ref, aj_ref, after_ref, out_ref):
+    del s_ref, after_ref
+    out_ref[...] = gram(ai_ref[...], aj_ref[...])
+
+
+def recip(x):
+    r = pl.reciprocal(x, approx=True)
+    return r * (2.0 - x * r)
+
+
+def lanes(x, c):
+    return jnp.broadcast_to(x[:, c : c + 1], (8, NB))
+
+
+def sublanes(x, k):
+    return jnp.broadcast_to(x[k : k + 1, :], (8, NB))
 
 
 def eliminate(T):
@@ -174,34 +186,50 @@
     lane = lax.broadcasted_iota(jnp.int32, (8, NB), 1)
     sub = lax.broadcasted_iota(jnp.int32, (8, NB), 0)
     out = [None] * n
+    own = [lanes(T[0], k) for k in range(8)]
     for g in range(n):
         c0 = 8 * g
-        V = [jnp.broadcast_to(T[g][:, c0 + k : c0 + k + 1], (8, NB)) for k in range(8)]
+        last = g == n - 1
+        V = list(own) + ([] if last else [lanes(T[g], c0 + 8 + k) for k in range(8)])
+        if not last:
+            A = [lanes(T[g + 1], c0 + k) for k in range(8)]
+            U = [lanes(T[g + 1], c0 + 8 + k) for k in range(8)]
         ingroup = (lane >= c0) & (lane < c0 + 8)
         R = jnp.where(ingroup, jnp.where(lane == sub + c0, 1.0, 0.0), T[g])
+        R1 = None if last else jnp.where(ingroup, 0.0, T[g + 1])
         rcp, d, rows = [], [], []
         pivot = jnp.ones((8, NB), F32)
         for k in range(8):
-            dk = [jnp.broadcast_to(V[j][k : k + 1, :], (8, NB)) for j in range(k, 8)]
-            r = 1.0 / dk[0]
+            dk = [sublanes(V[j], k) for j in range(k, len(V))]
+            r = recip(dk[0])
             pivot = jnp.where(sub == k, dk[0], pivot)
-            Rk = jnp.broadcast_to(R[k : k + 1, :], (8, NB))
+            Rk = sublanes(R, k)
             rcp.append(r)
             d.append(dk)
             rows.append(Rk)
             if k < 7:
-                m = jnp.where(sub > k, V[k] * r, 0.0)
-                for j in range(k + 1, 8):
+                m = jnp.where(sub > k, V[k], 0.0) * r
+                for j in range(k + 1, len(V)):
                     V[j] = V[j] - m * dk[j - k]
                 R = R - m * Rk
+            if not last:
+                m = A[k] * r
+                for j in range(k + 1, 8):
+                    A[j] = A[j] - m * dk[j - k]
+                for j in range(8):
+                    U[j] = U[j] - m * dk[8 + j - k]
+                R1 = R1 - m * Rk
         out[g] = jnp.where(lane < c0 + 8, R * lax.rsqrt(pivot), 0.0)
-        for s in range(g + 1, n):
-            V = [jnp.broadcast_to(T[s][:, c0 + k : c0 + k + 1], (8, NB)) for k in range(8)]
+        if not last:
+            T[g + 1] = R1
+            own = U
+        for s in range(g + 2, n):
+            W = [lanes(T[s], c0 + k) for k in range(8)]
             R = jnp.where(ingroup, 0.0, T[s])
             for k in range(8):
-                m = V[k] * rcp[k]
+                m = W[k] * rcp[k]
                 for j in range(k + 1, 8):
-                    V[j] = V[j] - m * d[k][j - k]
+                    W[j] = W[j] - m * d[k][j - k]
                 R = R - m * rows[k]
             T[s] = R
     return out
@@ -240,20 +268,42 @@
     def _():
         x_ref[0:16, :] = a_ref[pl.ds(pl.multiple_of(rank * 16, 16), 16), :]
 
+    def rest_of(b, o, inv):
+        xf = dot3(split(x_ref[:, o : o + NB]), inv, NT)
+        px_ref[:, o : o + NB] = xf
+        if b == n - 1:
+            return
+        near, far = slice(o + NB, o + 2 * NB), slice(o + 2 * NB, BS)
+        xf = split(xf)
+        X1 = split(c_ref[near, o : o + NB])
+        x_ref[:, near] = x_ref[:, near] - dot3(xf, X1, NT)
+        if b < n - 2:
+            X2 = dot3(split(a_ref[far, o : o + NB]), inv, NT)
+            c_ref[far, o : o + NB] = X2
+            X2 = split(X2)
+            a_ref[far, near] = a_ref[far, near] - dot3(X2, X1, NT)
+            a_ref[far, far] = a_ref[far, far] - dot3(X2, X2, NT)
+            x_ref[:, far] = x_ref[:, far] - dot3(xf, X2, NT)
+
+    T = [a_ref[8 * g : 8 * g + 8, 0:NB] for g in range(NB // 8)]
+    left = None
     for b in range(n):
         o = b * NB
-        out = eliminate([a_ref[o + 8 * g : o + 8 * g + 8, o : o + NB] for g in range(NB // 8)])
+        out = eliminate(T)
+        if left is not None:
+            rest_of(*left)
         for g in range(NB // 8):
             i_ref[b, 8 * g : 8 * g + 8, :] = out[g]
         inv = split(i_ref[b])
-        xf = dot3(split(x_ref[:, o : o + NB]), inv, NT)
-        px_ref[:, o : o + NB] = xf
         if b < n - 1:
-            X = dot3(split(a_ref[o + NB :, o : o + NB]), inv, NT)
-            c_ref[o + NB :, o : o + NB] = X
-            Xs = split(X)
-            a_ref[o + NB :, o + NB :] = a_ref[o + NB :, o + NB :] - dot3(Xs, Xs, NT)
-            x_ref[:, o + NB :] = x_ref[:, o + NB :] - dot3(split(xf), Xs, NT)
+            near = slice(o + NB, o + 2 * NB)
+            X1 = dot3(split(a_ref[near, o : o + NB]), inv, NT)
+            c_ref[near, o : o + NB] = X1
+            X1 = split(X1)
+            diagonal = a_ref[near, near] - dot3(X1, X1, NT)
+            T = [diagonal[8 * g : 8 * g + 8, :] for g in range(NB // 8)]
+        left = (b, o, inv)
+    rest_of(*left)
     panel = px_ref[0:16, :]
     grow = rank * 16 + lax.broadcasted_iota(jnp.int32, (16, BS), 0)
     gcol = lax.broadcasted_iota(jnp.int32, (16, BS), 1)
@@ -276,19 +326,20 @@
                 w_ref[:, q * NB : (q + 1) * NB] = wv[2 * half + q]
 
 
-def update_kernel(s_ref, w_ref, own_ref, r0_ref, r1_ref, r2_ref, mine_ref, other_ref):
+def update_kernel(s_ref, w_ref, own_ref, r0_ref, r1_ref, r2_ref, rest_ref, mine_ref, other_ref):
     core = s_ref[CORE]
     for e, recv_ref in enumerate((r0_ref, r1_ref, r2_ref)):
         own = s_ref[OWN + e]
+        cols = slice(e * BS, (e + 1) * BS)
         got = jnp.where(own == 1, own_ref[...], recv_ref[...])
         part = dot3(split(w_ref[16 * e : 16 * e + 16, :]), split(got), NT)
-        cols = slice(e * BS, (e + 1) * BS)
+        part = rest_ref[:, cols] - part
         low, high = part[0:8, :], part[8:16, :]
         mine_ref[:, cols] = jnp.where(core == 0, low, high)
         other_ref[:, cols] = jnp.where(core == 0, high, low)
 
 
-def finish_kernel(s_ref, panel_ref, rest_ref, mine_ref, other_ref, out_ref):
+def finish_kernel(s_ref, panel_ref, mine_ref, other_ref, out_ref):
     core = s_ref[CORE]
     row = s_ref[RANK] * 16 + core * 8 + lax.broadcasted_iota(jnp.int32, (8, BS), 0)
     col = lax.broadcasted_iota(jnp.int32, (8, BS), 1)
@@ -296,7 +347,7 @@
     values = []
     for e in range(3):
         cols = slice(e * BS, (e + 1) * BS)
-        value = (rest_ref[:, cols] - (mine_ref[:, cols] + other_ref[:, cols])) * (1.0 / TOKENS)
+        value = (mine_ref[:, cols] + other_ref[:, cols]) * (1.0 / TOKENS)
         on_diagonal = s_ref[ROW_I + 1 + e] == s_ref[COL_J + e]
         values.append(value + jnp.where(on_diagonal & (row == col), DAMPING, 0.0))
     for slot in range(4):
@@ -357,10 +408,9 @@
     first = mine + lax.ppermute(other, "dp", CORE_SWAP)
     over_z = exchange(first, Z_GROUPS)
 
-    wide = jax.ShapeDtypeStruct((BS // 2, 3 * BS), F32)
-    mine, other = pl.pallas_call(
+    both = pl.pallas_call(
         trailing_kernel,
-        out_shape=[wide, wide],
+        out_shape=jax.ShapeDtypeStruct((BS, 3 * BS), F32),
         grid_spec=pltpu.PrefetchScalarGridSpec(
             num_scalar_prefetch=1,
             grid=(3,),
@@ -369,23 +419,24 @@
                 pl.BlockSpec((tok, BS), lambda e, s: (0, s[COL_J + e])),
                 HBM,
             ],
-            out_specs=[pl.BlockSpec((BS // 2, BS), lambda e, s: (0, e))] * 2,
+            out_specs=pl.BlockSpec((BS, BS), lambda e, s: (0, e)),
         ),
         compiler_params=params(GRAM_LIMIT),
         cost_estimate=pl.CostEstimate(flops=4_000_000_000, bytes_accessed=7_000_000, transcendentals=0),
         name="trailing_gram",
     )(place, act, act, first)
-    both = mine + lax.ppermute(other, "dp", CORE_SWAP)
-    rest = lax.psum_scatter(both, "dp", scatter_dimension=0, tiled=True, axis_index_groups=Z_GROUPS)
-    rest = lax.psum_scatter(rest, "dp", scatter_dimension=0, tiled=True, axis_index_groups=Y_GROUPS)
+    both = after(both, over_z)
+    rest_z = lax.psum_scatter(both, "dp", scatter_dimension=0, tiled=True, axis_index_groups=Z_GROUPS)
+    rest = lax.psum_scatter(rest_z, "dp", scatter_dimension=0, tiled=True, axis_index_groups=Y_GROUPS)
 
     spread = pl.pallas_call(
         sum_z_kernel,
         out_shape=jax.ShapeDtypeStruct((NY, 72, HALF), F32),
-        in_specs=vmem(1) + [HBM],
+        in_specs=vmem(1),
         out_specs=vmem(1)[0],
+        compiler_params=params(),
         name="sum_over_z",
-    )(over_z, other)
+    )(over_z)
     over_y = exchange(spread, Y_GROUPS)
     corner_rows, held_rows, own_rows = pl.pallas_call(
         sum_y_kernel,
@@ -394,17 +445,19 @@
             jax.ShapeDtypeStruct((NZ, 64, HALF), F32),
             jax.ShapeDtypeStruct((16, HALF), F32),
         ],
-        in_specs=[SMEM] + vmem(1) + [HBM],
+        in_specs=[SMEM] + vmem(1),
         out_specs=vmem(3),
+        compiler_params=params(),
         name="sum_over_y",
-    )(place, over_y, both)
+    )(place, over_y)
 
     corner_rows = exchange(corner_rows, Z_GROUPS)
     column = exchange(held_rows, Z_GROUPS).reshape(BS, HALF)
     share = jnp.concatenate([corner_rows.reshape(64, HALF), own_rows], axis=0)
     share = lax.all_to_all(jnp.broadcast_to(share, (NBLK, 80, HALF)), "blk", 0, 0)
     share_other = lax.ppermute(share, "dp", CORE_SWAP)
-    brought = [lax.ppermute(column, "blk", list(pairs)) for pairs in ROUNDS]
+    sent = after(column, rest_z)
+    brought = [lax.ppermute(sent, "blk", list(pairs)) for pairs in ROUNDS]
 
     panel, w = pl.pallas_call(
         corner_kernel,
@@ -427,18 +480,19 @@
     mine, other = pl.pallas_call(
         update_kernel,
         out_shape=[part, part],
-        in_specs=[SMEM] + vmem(5),
+        in_specs=[SMEM] + vmem(6),
         out_specs=vmem(2),
         compiler_params=params(),
         name="update",
-    )(place, w, column, *brought)
+    )(place, w, sent, *brought, rest)
     return pl.pallas_call(
         finish_kernel,
         out_shape=jax.ShapeDtypeStruct((8, 4 * BS), F32),
-        in_specs=[SMEM] + vmem(4),
+        in_specs=[SMEM] + vmem(3),
         out_specs=vmem(1)[0],
+        compiler_params=params(),
         name="finish",
-    )(place, panel, rest, mine, lax.ppermute(other, "dp", CORE_SWAP))
+    )(place, panel, mine, lax.ppermute(other, "dp", CORE_SWAP))
 
 
 def solution(mesh):

time: 170 us -> 163 us (0.959)
  the two profiles are of different devices: /device:TPU:1 before, /device:TPU:19 now
where the time goes in v2:
time: 163 us; the launch traced here: 162 us
  blocking collectives  40.3 us (25%)
  starting transfers between devices  37.9 us (23%)
  waiting for transfers between devices  32.1 us (20%)
  Pallas kernels  31.9 us (20%)
  between operations  13.5 us (8%)
  local copies, waits for them, and re-layouts  4.81 us (3%)
  other arithmetic  1.97 us (1%)
    all_to_all x2, blocking collectives, exchange(): return lax.all_to_all(x, 'dp', 0, 0, axis_index_groups=groups)  28.1 us
    all_to_all x2, waiting for transfers between devices, exchange(): return lax.all_to_all(x, 'dp', 0, 0, axis_index_groups=groups)  22.1 us
    pallas_call x1, Pallas kernels, body(): pl.pallas_call(corner_kernel, out_shape=[jax.ShapeDtypeStruct((16, BS), F...  16.9 us
    all_to_all x2, starting transfers between devices, exchange(): return lax.all_to_all(x, 'dp', 0, 0, axis_index_groups=groups)  13.5 us
    all_to_all x1, blocking collectives, body(): lax.all_to_all(jnp.broadcast_to(share, (NBLK, 80, HALF)), 'blk', 0, 0)  12.2 us
    ppermute x3, starting transfers between devices, body(): brought = [lax.ppermute(sent, 'blk', list(pairs)) for pairs in ROUNDS]  9.72 us
    ppermute x3, waiting for transfers between devices, body(): brought = [lax.ppermute(sent, 'blk', list(pairs)) for pairs in ROUNDS]  7.22 us
    ppermute x1, starting transfers between devices, body(): lax.ppermute(other, 'dp', CORE_SWAP)  7.05 us
  transfers between devices with their start and end apart: 10, of which 5 were waited for; matrix products, arithmetic and copies ran while one was open for 0% of the time, Pallas kernels for 15%

profile of v2, /device:TPU:19, one launch (start us, length us, event | category | flops | bytes accessed | tf_op | source)
XLA Modules:
  0.0 162.4 jit_solution(439559040166492691)
XLA Ops:
  6.5 1.2 dynamic-slice_bitcast_fusion.s_ref
  7.7 4.7 %first_column.1 = (f32[8,72,256]{2,1,0:T(8,128)}, f32[8,72,256]{2,1,0:T(8,128)}) custom-call(s32[24]{0:T(128)} %dynamic-slice_bitcast_fusion.s_ref, bf16[640,3584]{1,0:T(8,128)(2,1)} %aj_ref.1, bf16[640,3584]{1,0:T(8,128)(2,1)} %aj_ref.1), custom_call_target="tpu_custom_call" | custom-call | tf_op jit(solution)/shard_map/first_column/pallas_call | solution.py:392
  12.4 2.6 %collective-permute-start = (f32[8,72,256]{2,1,0:T(8,128)}, f32[8,72,256]{2,1,0:T(8,128)S(1)}, u32[]{:S(2)}, u32[]{:S(2)}) collective-permute-start(f32[8,72,256]{2,1,0:T(8,128)} %get-tuple-element.15), channel_id=1, source_target_pairs={{0,8},{8,0},{16,24},{24,16},{32,40},{40,32},{48,56},{56,48},{64,72... | collective-permute-start | bytes 1769480 | tf_op jit(solution)/shard_map/ppermute | solution.py:408
  15.0 1.8 %collective-permute-done = f32[8,72,256]{2,1,0:T(8,128)S(1)} collective-permute-done((f32[8,72,256]{2,1,0:T(8,128)}, f32[8,72,256]{2,1,0:T(8,128)S(1)}, u32[]{:S(2)}, u32[]{:S(2)}) %collective-permute-start) | collective-permute-done | bytes 589856 | tf_op jit(solution)/shard_map/ppermute | solution.py:408
  16.8 2.0 %add.16.after_ref = f32[8,72,256]{2,1,0:T(8,128)} add(f32[8,72,256]{2,1,0:T(8,128)} %get-tuple-element.14, f32[8,72,256]{2,1,0:T(8,128)S(1)} %collective-permute-done) | non-fusion elementwise | flops 147456 | bytes 1769472 | tf_op jit(solution)/shard_map/add | solution.py:408
  18.7 10.0 %all-to-all-start = ((f32[8,72,256]{2,1,0:T(8,128)}), f32[8,72,256]{2,1,0:T(8,128)S(1)}, u32[]{:S(2)}, u32[]{:S(2)}) async-start(f32[8,72,256]{2,1,0:T(8,128)} %add.16.after_ref), calls=%async_computation | async-start | bytes 1179648 | tf_op jit(solution)/shard_map/all_to_all | solution.py:381
  28.8 0.0 reduce-scatter.3.cloned.1.call-start
  28.8 6.4 %trailing_gram.1.x_ref = f32[512,1536]{1,0:T(8,128)} custom-call(s32[24]{0:T(128)} %dynamic-slice_bitcast_fusion.s_ref, bf16[640,3584]{1,0:T(8,128)(2,1)} %aj_ref.1, bf16[640,3584]{1,0:T(8,128)(2,1)} %aj_ref.1, f32[8,72,256]{2,1,0:T(8,128)} %add.16.after_ref), custom_call_target="tpu_custom_call" | custom-call | flops 4000000000 | bytes 7000000 | tf_op jit(solution)/shard_map/trailing_gram/pallas_call | solution.py:411
  35.3 12.9 %all-to-all-done.x_ref.after_ref = f32[8,72,256]{2,1,0:T(8,128)S(1)} async-done(((f32[8,72,256]{2,1,0:T(8,128)}), f32[8,72,256]{2,1,0:T(8,128)S(1)}, u32[]{:S(2)}, u32[]{:S(2)}) %all-to-all-start) | async-done | bytes 589856 | tf_op jit(solution)/shard_map/all_to_all | solution.py:381
  48.2 0.8 copy-done
  49.0 0.0 reduce-scatter.3.cloned.1.call-update
  49.0 1.0 copy-done.1
  50.1 17.3 %all_to_all.25.x_ref = f32[4,72,256]{2,1,0:T(8,128)S(1)} all-to-all(f32[4,72,256]{2,1,0:T(8,128)S(1)} %sum_over_z.1), channel_id=1, replica_groups={{0,16,32,48},{8,24,40,56},{64,80,96,112},{72,88,104,120},{128,144,160,1..., dimensions={0} | all-to-all | bytes 589824 | tf_op jit(solution)/shard_map/all_to_all | solution.py:381
  67.4 1.4 sum_over_y.1
  68.8 10.8 %all_to_all.26 = f32[8,8,256]{2,1,0:T(8,128)S(1)} all-to-all(f32[8,8,256]{2,1,0:T(8,128)S(1)} %get-tuple-element.16), channel_id=1, replica_groups={{0,64,128,192,256,320,384,448},{8,72,136,200,264,328,392,456},{16,80,14..., dimensions={0} | all-to-all | bytes 131072 | tf_op jit(solution)/shard_map/all_to_all | solution.py:381
  79.7 12.2 %all_to_all.27.mine_ref = f32[8,80,256]{2,1,0:T(8,128)S(1)} all-to-all(f32[8,80,256]{2,1,0:T(8,128)S(1)} %broadcast_in_dim.3), channel_id=1, replica_groups=mesh['dp'=64,'blk'=8] {'blk'}, dimensions={0} | all-to-all | bytes 1310720 | tf_op jit(solution)/shard_map/all_to_all | solution.py:457
  91.8 3.5 %all-to-all-start.4 = ((f32[8,64,256]{2,1,0:T(8,128)}), f32[8,64,256]{2,1,0:T(8,128)S(1)}, u32[]{:S(2)}, u32[]{:S(2)}) async-start(f32[8,64,256]{2,1,0:T(8,128)} %get-tuple-element.20), calls=%async_computation.4 | async-start | bytes 1048576 | tf_op jit(solution)/shard_map/all_to_all | solution.py:381
  95.3 0.0 reduce-scatter.5.cloned.1.call-start
  95.4 5.0 %collective-permute-start.1 = (f32[8,80,256]{2,1,0:T(8,128)S(1)}, f32[8,80,256]{2,1,0:T(8,128)S(1)}, u32[]{:S(2)}, u32[]{:S(2)}) collective-permute-start(f32[8,80,256]{2,1,0:T(8,128)S(1)} %all_to_all.27.mine_ref), channel_id=1, source_target_pairs={{0,8},{8,0},{16,24},{24,16},{32,40},{40,32},{48,56},{56,48},{64,72... | collective-permute-start | bytes 1966088 | tf_op jit(solution)/shard_map/ppermute | solution.py:458
  100.3 9.2 %all-to-all-done.4 = f32[8,64,256]{2,1,0:T(8,128)S(1)} async-done(((f32[8,64,256]{2,1,0:T(8,128)}), f32[8,64,256]{2,1,0:T(8,128)S(1)}, u32[]{:S(2)}, u32[]{:S(2)}) %all-to-all-start.4) | async-done | bytes 524320 | tf_op jit(solution)/shard_map/all_to_all | solution.py:381
  109.6 0.8 copy-done.2
  110.4 3.2 %collective-permute-start.2 = (f32[512,256]{1,0:T(8,128)}, f32[512,256]{1,0:T(8,128)S(1)}, u32[]{:S(2)}, u32[]{:S(2)}) collective-permute-start(f32[512,256]{1,0:T(8,128)} %after.3.own_ref), channel_id=1, source_target_pairs={{3,2},{4,0},{5,1},{6,3},{7,4},{2,5},{0,7},{11,10},{12,8},{13,9},{1... | collective-permute-start | bytes 1572872 | tf_op jit(solution)/shard_map/ppermute | solution.py:460
  113.6 1.3 collective-permute-start.3
  114.9 5.2 %collective-permute-start.4 = (f32[512,256]{1,0:T(8,128)}, f32[512,256]{1,0:T(8,128)S(1)}, u32[]{:S(2)}, u32[]{:S(2)}) collective-permute-start(f32[512,256]{1,0:T(8,128)} %after.3.own_ref), channel_id=1, source_target_pairs={{3,5},{4,7},{1,2},{2,6},{11,13},{12,15},{9,10},{10,14},{19,21},{20... | collective-permute-start | bytes 1572872 | tf_op jit(solution)/shard_map/ppermute | solution.py:460
  120.1 0.0 reduce-scatter.5.cloned.1.call-update
  120.2 16.9 %corner.1 = (f32[16,512]{1,0:T(8,128)S(1)}, f32[48,256]{1,0:T(8,128)S(1)}) custom-call(s32[24]{0:T(128)S(1)} %copy-done.5, f32[8,80,256]{2,1,0:T(8,128)S(1)} %all_to_all.27.mine_ref, f32[8,80,256]{2,1,0:T(8,128)S(1)} %collective-permute-done.1.other_ref), custom_call_target="tpu_custom_call" | custom-call | flops 20000000000 | bytes 2000000 | tf_op jit(solution)/shard_map/corner/pallas_call | solution.py:462
  137.1 7.2 %collective-permute-done.4.r2_ref = f32[512,256]{1,0:T(8,128)S(1)} collective-permute-done((f32[512,256]{1,0:T(8,128)}, f32[512,256]{1,0:T(8,128)S(1)}, u32[]{:S(2)}, u32[]{:S(2)}) %collective-permute-start.4) | collective-permute-done | bytes 524320 | tf_op jit(solution)/shard_map/ppermute | solution.py:460
  144.3 0.9 copy-done.4
  145.2 1.3 update.1
  146.5 7.0 %collective-permute-start.5 = (f32[8,1536]{1,0:T(8,128)S(1)}, f32[8,1536]{1,0:T(8,128)S(1)}, u32[]{:S(2)}, u32[]{:S(2)}) collective-permute-start(f32[8,1536]{1,0:T(8,128)S(1)} %get-tuple-element.22), channel_id=1, source_target_pairs={{0,8},{8,0},{16,24},{24,16},{32,40},{40,32},{48,56},{56,48},{64,72... | collective-permute-start | bytes 147464 | tf_op jit(solution)/shard_map/ppermute | solution.py:495
  153.6 0.9 collective-permute-done.5.other_ref
  154.4 1.2 finish.1
  (18 shorter events, 0.1 us)
Async XLA Ops:
  12.4 4.4 %collective-permute-start = (f32[8,72,256]{2,1,0:T(8,128)}, f32[8,72,256]{2,1,0:T(8,128)S(1)}, u32[]{:S(2)}, u32[]{:S(2)}) collective-permute-start(f32[8,72,256]{2,1,0:T(8,128)} %get-tuple-element.15), channel_id=1, source_target_pairs={{0,8},{8,0},{16,24},{24,16},{32,40},{40,32},{48,56},{56,48},{64,72... | collective-permute-start | bytes 1769480 | tf_op jit(solution)/shard_map/ppermute | solution.py:408
  18.7 29.4 %all-to-all-start = ((f32[8,72,256]{2,1,0:T(8,128)}), f32[8,72,256]{2,1,0:T(8,128)S(1)}, u32[]{:S(2)}, u32[]{:S(2)}) async-start(f32[8,72,256]{2,1,0:T(8,128)} %add.16.after_ref), calls=%async_computation | async-start | bytes 1179648 | tf_op jit(solution)/shard_map/all_to_all | solution.py:381
  28.8 80.8 %reduce-scatter.3.cloned.1.call-start = ((), (), s32[]{:S(2)}) async-start(), calls=%async_computation.7 | async-start | bytes 3538944 | tf_op jit(solution)/shard_map/reduce_scatter | solution.py:429
  48.2 0.8 copy-start
  49.0 1.1 copy-start.1
  49.0 18.4 %copy-start.5 = (s32[24]{0:T(128)S(1)}, s32[24]{0:T(128)}, u32[]{:S(2)}) copy-start(s32[24]{0:T(128)} %dynamic-slice_bitcast_fusion.s_ref) | copy-start | bytes 292
  91.8 17.8 %all-to-all-start.4 = ((f32[8,64,256]{2,1,0:T(8,128)}), f32[8,64,256]{2,1,0:T(8,128)S(1)}, u32[]{:S(2)}, u32[]{:S(2)}) async-start(f32[8,64,256]{2,1,0:T(8,128)} %get-tuple-element.20), calls=%async_computation.4 | async-start | bytes 1048576 | tf_op jit(solution)/shard_map/all_to_all | solution.py:381
  95.3 49.0 %reduce-scatter.5.cloned.1.call-start = ((), (), s32[]{:S(2)}) async-start(), calls=%async_computation.8 | async-start | bytes 491520 | tf_op jit(solution)/shard_map/reduce_scatter | solution.py:430
  95.4 24.8 %collective-permute-start.1 = (f32[8,80,256]{2,1,0:T(8,128)S(1)}, f32[8,80,256]{2,1,0:T(8,128)S(1)}, u32[]{:S(2)}, u32[]{:S(2)}) collective-permute-start(f32[8,80,256]{2,1,0:T(8,128)S(1)} %all_to_all.27.mine_ref), channel_id=1, source_target_pairs={{0,8},{8,0},{16,24},{24,16},{32,40},{40,32},{48,56},{56,48},{64,72... | collective-permute-start | bytes 1966088 | tf_op jit(solution)/shard_map/ppermute | solution.py:458
  109.6 0.8 copy-start.2
  110.4 26.7 %collective-permute-start.2 = (f32[512,256]{1,0:T(8,128)}, f32[512,256]{1,0:T(8,128)S(1)}, u32[]{:S(2)}, u32[]{:S(2)}) collective-permute-start(f32[512,256]{1,0:T(8,128)} %after.3.own_ref), channel_id=1, source_target_pairs={{3,2},{4,0},{5,1},{6,3},{7,4},{2,5},{0,7},{11,10},{12,8},{13,9},{1... | collective-permute-start | bytes 1572872 | tf_op jit(solution)/shard_map/ppermute | solution.py:460
  113.6 23.5 %collective-permute-start.3 = (f32[512,256]{1,0:T(8,128)}, f32[512,256]{1,0:T(8,128)S(1)}, u32[]{:S(2)}, u32[]{:S(2)}) collective-permute-start(f32[512,256]{1,0:T(8,128)} %after.3.own_ref), channel_id=1, source_target_pairs={{3,4},{4,6},{5,2},{1,0},{7,3},{0,1},{11,12},{12,14},{13,10},{9,8},... | collective-permute-start | bytes 1572872 | tf_op jit(solution)/shard_map/ppermute | solution.py:460
  114.9 29.4 %collective-permute-start.4 = (f32[512,256]{1,0:T(8,128)}, f32[512,256]{1,0:T(8,128)S(1)}, u32[]{:S(2)}, u32[]{:S(2)}) collective-permute-start(f32[512,256]{1,0:T(8,128)} %after.3.own_ref), channel_id=1, source_target_pairs={{3,5},{4,7},{1,2},{2,6},{11,13},{12,15},{9,10},{10,14},{19,21},{20... | collective-permute-start | bytes 1572872 | tf_op jit(solution)/shard_map/ppermute | solution.py:460
  120.1 24.2 %copy-start.3 = (f32[512,256]{1,0:T(8,128)S(1)}, f32[512,256]{1,0:T(8,128)}, u32[]{:S(2)}) copy-start(f32[512,256]{1,0:T(8,128)} %after.3.own_ref) | copy-start | bytes 1572868
  144.3 0.9 copy-start.4
  146.5 7.9 %collective-permute-start.5 = (f32[8,1536]{1,0:T(8,128)S(1)}, f32[8,1536]{1,0:T(8,128)S(1)}, u32[]{:S(2)}, u32[]{:S(2)}) collective-permute-start(f32[8,1536]{1,0:T(8,128)S(1)} %get-tuple-element.22), channel_id=1, source_target_pairs={{0,8},{8,0},{16,24},{24,16},{32,40},{40,32},{48,56},{56,48},{64,72... | collective-permute-start | bytes 147464 | tf_op jit(solution)/shard_map/ppermute | solution.py:495
Sparse Core Ops, SparseCore 0:
  49.1 44.7 reduce-scatter.2
  120.3 22.4 reduce-scatter.4

commit v3 on v2

--- a/solution.py
+++ b/solution.py
@@ -15,7 +15,7 @@
 F32 = jnp.float32
 VMEM_LIMIT = 40 * 1024 * 1024
 GRAM_LIMIT = 60 * 1024 * 1024
-CORNER_FLOPS = 20_000_000_000
+CORNER_FLOPS = 200000000
 
 HELD = (2, 1, 2, 3, 4, 5, 6, 1)
 TRAIL = (
@@ -122,7 +122,8 @@
             store(other_ref)
 
 
-def sum_z_kernel(x_ref, out_ref):
+def sum_z_kernel(x_ref, out_ref, ready_ref):
+    ready_ref[...] = jnp.zeros(ready_ref.shape, F32)
     total = x_ref[0]
     for z in range(1, NZ):
         total = total + x_ref[z]
@@ -151,11 +152,11 @@
 HBM = pl.BlockSpec(memory_space=pltpu.HBM)
 
 
-def after(x, dep):
+def after(x, dep, where=HBM):
     return pl.pallas_call(
         pass_kernel,
         out_shape=jax.ShapeDtypeStruct(x.shape, x.dtype),
-        in_specs=[HBM, HBM],
+        in_specs=[HBM, where],
         out_specs=HBM,
         input_output_aliases={0: 0},
         name="after",
@@ -425,18 +426,17 @@
         cost_estimate=pl.CostEstimate(flops=4_000_000_000, bytes_accessed=7_000_000, transcendentals=0),
         name="trailing_gram",
     )(place, act, act, first)
-    both = after(both, over_z)
-    rest_z = lax.psum_scatter(both, "dp", scatter_dimension=0, tiled=True, axis_index_groups=Z_GROUPS)
-    rest = lax.psum_scatter(rest_z, "dp", scatter_dimension=0, tiled=True, axis_index_groups=Y_GROUPS)
-
-    spread = pl.pallas_call(
+    spread, ready = pl.pallas_call(
         sum_z_kernel,
-        out_shape=jax.ShapeDtypeStruct((NY, 72, HALF), F32),
+        out_shape=[jax.ShapeDtypeStruct((NY, 72, HALF), F32), jax.ShapeDtypeStruct((8, NB), F32)],
         in_specs=vmem(1),
-        out_specs=vmem(1)[0],
+        out_specs=vmem(2),
         compiler_params=params(),
         name="sum_over_z",
     )(over_z)
+    both = after(both, ready, vmem(1)[0])
+    rest_z = lax.psum_scatter(both, "dp", scatter_dimension=0, tiled=True, axis_index_groups=Z_GROUPS)
+    rest = lax.psum_scatter(rest_z, "dp", scatter_dimension=0, tiled=True, axis_index_groups=Y_GROUPS)
     over_y = exchange(spread, Y_GROUPS)
     corner_rows, held_rows, own_rows = pl.pallas_call(
         sum_y_kernel,
@@ -455,9 +455,9 @@
     column = exchange(held_rows, Z_GROUPS).reshape(BS, HALF)
     share = jnp.concatenate([corner_rows.reshape(64, HALF), own_rows], axis=0)
     share = lax.all_to_all(jnp.broadcast_to(share, (NBLK, 80, HALF)), "blk", 0, 0)
+    share = after(share, rest_z)
     share_other = lax.ppermute(share, "dp", CORE_SWAP)
-    sent = after(column, rest_z)
-    brought = [lax.ppermute(sent, "blk", list(pairs)) for pairs in ROUNDS]
+    brought = [lax.ppermute(column, "blk", list(pairs)) for pairs in ROUNDS]
 
     panel, w = pl.pallas_call(
         corner_kernel,
@@ -484,7 +484,7 @@
         out_specs=vmem(2),
         compiler_params=params(),
         name="update",
-    )(place, w, sent, *brought, rest)
+    )(place, w, column, *brought, rest)
     return pl.pallas_call(
         finish_kernel,
         out_shape=jax.ShapeDtypeStruct((8, 4 * BS), F32),

time: 163 us -> 161 us (0.988)
  starting transfers between devices: 37.9 us -> 35.4 us
    ppermute x1, starting transfers between devices: 7.05 us -> 4.33 us  [body(): lax.ppermute(other, 'dp', CORE_SWAP)]
    unnamed x12 -> x8, local copies, waits for them, and re-layouts: 3.56 us -> 2.56 us
where the time goes in v3:
time: 161 us; the launch traced here: 160 us
  blocking collectives  40.3 us (25%)
  starting transfers between devices  35.4 us (22%)
  Pallas kernels  32.6 us (20%)
  waiting for transfers between devices  32.4 us (20%)
  between operations  13.5 us (8%)
  local copies, waits for them, and re-layouts  3.88 us (2%)
  other arithmetic  1.96 us (1%)
    all_to_all x2, blocking collectives, exchange(): return lax.all_to_all(x, 'dp', 0, 0, axis_index_groups=groups)  28.1 us
    all_to_all x2, waiting for transfers between devices, exchange(): return lax.all_to_all(x, 'dp', 0, 0, axis_index_groups=groups)  21.2 us
    pallas_call x1, Pallas kernels, body(): pl.pallas_call(corner_kernel, out_shape=[jax.ShapeDtypeStruct((16, BS), F...  16.9 us
    all_to_all x2, starting transfers between devices, exchange(): return lax.all_to_all(x, 'dp', 0, 0, axis_index_groups=groups)  13.5 us
    all_to_all x1, blocking collectives, body(): lax.all_to_all(jnp.broadcast_to(share, (NBLK, 80, HALF)), 'blk', 0, 0)  12.2 us
    ppermute x3, starting transfers between devices, body(): brought = [lax.ppermute(column, 'blk', list(pairs)) for pairs in ROUNDS]  9.8 us
    ppermute x3, waiting for transfers between devices, body(): brought = [lax.ppermute(column, 'blk', list(pairs)) for pairs in ROUNDS]  7.78 us
    pallas_call x1, Pallas kernels, body(): pl.pallas_call(trailing_kernel, out_shape=jax.ShapeDtypeStruct((BS, 3 * B...  6.42 us
  transfers between devices with their start and end apart: 10, of which 5 were waited for; matrix products, arithmetic and copies ran while one was open for 0% of the time, Pallas kernels for 15%

profile of v3, /device:TPU:19, one launch (start us, length us, event | category | flops | bytes accessed | tf_op | source)
XLA Modules:
  0.0 160.0 jit_solution(6781495419535812903)
XLA Ops:
  6.5 1.3 dynamic-slice_bitcast_fusion.s_ref
  7.8 4.7 %first_column.1 = (f32[8,72,256]{2,1,0:T(8,128)}, f32[8,72,256]{2,1,0:T(8,128)}) custom-call(s32[24]{0:T(128)} %dynamic-slice_bitcast_fusion.s_ref, bf16[640,3584]{1,0:T(8,128)(2,1)} %aj_ref.1, bf16[640,3584]{1,0:T(8,128)(2,1)} %aj_ref.1), custom_call_target="tpu_custom_call" | custom-call | tf_op jit(solution)/shard_map/first_column/pallas_call | solution.py:393
  12.5 2.6 %collective-permute-start = (f32[8,72,256]{2,1,0:T(8,128)}, f32[8,72,256]{2,1,0:T(8,128)S(1)}, u32[]{:S(2)}, u32[]{:S(2)}) collective-permute-start(f32[8,72,256]{2,1,0:T(8,128)} %get-tuple-element.17), channel_id=1, source_target_pairs={{0,8},{8,0},{16,24},{24,16},{32,40},{40,32},{48,56},{56,48},{64,72... | collective-permute-start | bytes 1769480 | tf_op jit(solution)/shard_map/ppermute | solution.py:409
  15.0 1.8 %collective-permute-done = f32[8,72,256]{2,1,0:T(8,128)S(1)} collective-permute-done((f32[8,72,256]{2,1,0:T(8,128)}, f32[8,72,256]{2,1,0:T(8,128)S(1)}, u32[]{:S(2)}, u32[]{:S(2)}) %collective-permute-start) | collective-permute-done | bytes 589856 | tf_op jit(solution)/shard_map/ppermute | solution.py:409
  16.8 2.0 %add.16.after_ref = f32[8,72,256]{2,1,0:T(8,128)} add(f32[8,72,256]{2,1,0:T(8,128)} %get-tuple-element.16, f32[8,72,256]{2,1,0:T(8,128)S(1)} %collective-permute-done) | non-fusion elementwise | flops 147456 | bytes 1769472 | tf_op jit(solution)/shard_map/add | solution.py:409
  18.8 10.0 %all-to-all-start = ((f32[8,72,256]{2,1,0:T(8,128)}), f32[8,72,256]{2,1,0:T(8,128)S(1)}, u32[]{:S(2)}, u32[]{:S(2)}) async-start(f32[8,72,256]{2,1,0:T(8,128)} %add.16.after_ref), calls=%async_computation | async-start | bytes 1179648 | tf_op jit(solution)/shard_map/all_to_all | solution.py:382
  28.8 0.0 reduce-scatter.3.cloned.1.call-start
  28.9 6.4 %trailing_gram.1.x_ref = f32[512,1536]{1,0:T(8,128)} custom-call(s32[24]{0:T(128)} %dynamic-slice_bitcast_fusion.s_ref, bf16[640,3584]{1,0:T(8,128)(2,1)} %aj_ref.1, bf16[640,3584]{1,0:T(8,128)(2,1)} %aj_ref.1, f32[8,72,256]{2,1,0:T(8,128)} %add.16.after_ref), custom_call_target="tpu_custom_call" | custom-call | flops 4000000000 | bytes 7000000 | tf_op jit(solution)/shard_map/trailing_gram/pallas_call | solution.py:412
  35.3 12.9 %all-to-all-done.x_ref = f32[8,72,256]{2,1,0:T(8,128)S(1)} async-done(((f32[8,72,256]{2,1,0:T(8,128)}), f32[8,72,256]{2,1,0:T(8,128)S(1)}, u32[]{:S(2)}, u32[]{:S(2)}) %all-to-all-start) | async-done | bytes 589856 | tf_op jit(solution)/shard_map/all_to_all | solution.py:382
  48.3 0.6 copy-done.3
  48.8 0.7 after.2
  49.6 17.3 %all_to_all.25.x_ref = f32[4,72,256]{2,1,0:T(8,128)S(1)} all-to-all(f32[4,72,256]{2,1,0:T(8,128)S(1)} %get-tuple-element.18), channel_id=1, replica_groups={{0,16,32,48},{8,24,40,56},{64,80,96,112},{72,88,104,120},{128,144,160,1..., dimensions={0} | all-to-all | bytes 589824 | tf_op jit(solution)/shard_map/all_to_all | solution.py:382
  66.8 1.4 sum_over_y.1
  68.2 10.8 %all_to_all.26 = f32[8,8,256]{2,1,0:T(8,128)S(1)} all-to-all(f32[8,8,256]{2,1,0:T(8,128)S(1)} %get-tuple-element.19), channel_id=1, replica_groups={{0,64,128,192,256,320,384,448},{8,72,136,200,264,328,392,456},{16,80,14..., dimensions={0} | all-to-all | bytes 131072 | tf_op jit(solution)/shard_map/all_to_all | solution.py:382
  79.1 12.2 %all_to_all.27.x_ref = f32[8,80,256]{2,1,0:T(8,128)} all-to-all(f32[8,80,256]{2,1,0:T(8,128)S(1)} %broadcast_in_dim.3), channel_id=1, replica_groups=mesh['dp'=64,'blk'=8] {'blk'}, dimensions={0} | all-to-all | bytes 1310720 | tf_op jit(solution)/shard_map/all_to_all | solution.py:457
  91.3 3.5 %all-to-all-start.4 = ((f32[8,64,256]{2,1,0:T(8,128)}), f32[8,64,256]{2,1,0:T(8,128)S(1)}, u32[]{:S(2)}, u32[]{:S(2)}) async-start(f32[8,64,256]{2,1,0:T(8,128)} %get-tuple-element.24), calls=%async_computation.5 | async-start | bytes 1048576 | tf_op jit(solution)/shard_map/all_to_all | solution.py:382
  94.8 0.0 reduce-scatter.5.cloned.1.call-start
  94.8 0.0 reduce-scatter.3.cloned.1.call-done.after_ref
  94.9 0.7 reduce-scatter.5.cloned.1.call-update
  95.5 5.1 %collective-permute-start.1 = (f32[8,80,256]{2,1,0:T(8,128)}, f32[8,80,256]{2,1,0:T(8,128)S(1)}, u32[]{:S(2)}, u32[]{:S(2)}) collective-permute-start(f32[8,80,256]{2,1,0:T(8,128)} %after.3.mine_ref), channel_id=1, source_target_pairs={{0,8},{8,0},{16,24},{24,16},{32,40},{40,32},{48,56},{56,48},{64,72... | collective-permute-start | bytes 1966088 | tf_op jit(solution)/shard_map/ppermute | solution.py:459
  100.7 8.3 %all-to-all-done.4 = f32[8,64,256]{2,1,0:T(8,128)S(1)} async-done(((f32[8,64,256]{2,1,0:T(8,128)}), f32[8,64,256]{2,1,0:T(8,128)S(1)}, u32[]{:S(2)}, u32[]{:S(2)}) %all-to-all-start.4) | async-done | bytes 524320 | tf_op jit(solution)/shard_map/all_to_all | solution.py:382
  109.0 3.5 %collective-permute-start.2 = (f32[512,256]{1,0:T(8,128)S(1)}, f32[512,256]{1,0:T(8,128)S(1)}, u32[]{:S(2)}, u32[]{:S(2)}) collective-permute-start(f32[512,256]{1,0:T(8,128)S(1)} %bitcast.4), channel_id=1, source_target_pairs={{3,2},{4,0},{5,1},{6,3},{7,4},{2,5},{0,7},{11,10},{12,8},{13,9},{1... | collective-permute-start | bytes 1572872 | tf_op jit(solution)/shard_map/ppermute | solution.py:460
  112.4 1.3 collective-permute-start.3
  113.7 5.0 %collective-permute-start.4 = (f32[512,256]{1,0:T(8,128)S(1)}, f32[512,256]{1,0:T(8,128)S(1)}, u32[]{:S(2)}, u32[]{:S(2)}) collective-permute-start(f32[512,256]{1,0:T(8,128)S(1)} %bitcast.6), channel_id=1, source_target_pairs={{3,5},{4,7},{1,2},{2,6},{11,13},{12,15},{9,10},{10,14},{19,21},{20... | collective-permute-start | bytes 1572872 | tf_op jit(solution)/shard_map/ppermute | solution.py:460
  118.8 1.1 copy-done
  119.9 16.9 %corner.1 = (f32[16,512]{1,0:T(8,128)S(1)}, f32[48,256]{1,0:T(8,128)S(1)}) custom-call(s32[24]{0:T(128)S(1)} %copy-done.2, f32[8,80,256]{2,1,0:T(8,128)S(1)} %copy-done, f32[8,80,256]{2,1,0:T(8,128)S(1)} %collective-permute-done.1.other_ref), custom_call_target="tpu_custom_call" | custom-call | flops 200000000 | bytes 2000000 | tf_op jit(solution)/shard_map/corner/pallas_call | solution.py:462
  136.8 7.8 %collective-permute-done.4.r2_ref = f32[512,256]{1,0:T(8,128)S(1)} collective-permute-done((f32[512,256]{1,0:T(8,128)S(1)}, f32[512,256]{1,0:T(8,128)S(1)}, u32[]{:S(2)}, u32[]{:S(2)}) %collective-permute-start.4) | collective-permute-done | bytes 524320 | tf_op jit(solution)/shard_map/ppermute | solution.py:460
  144.6 0.9 copy-done.1
  145.5 1.3 update.1
  146.8 4.3 %collective-permute-start.5 = (f32[8,1536]{1,0:T(8,128)S(1)}, f32[8,1536]{1,0:T(8,128)S(1)}, u32[]{:S(2)}, u32[]{:S(2)}) collective-permute-start(f32[8,1536]{1,0:T(8,128)S(1)} %get-tuple-element.26), channel_id=1, source_target_pairs={{0,8},{8,0},{16,24},{24,16},{32,40},{40,32},{48,56},{56,48},{64,72... | collective-permute-start | bytes 147464 | tf_op jit(solution)/shard_map/ppermute | solution.py:495
  151.1 0.9 collective-permute-done.5.other_ref
  152.0 1.2 finish.1
  (14 shorter events, 0.1 us)
Async XLA Ops:
  12.5 4.4 %collective-permute-start = (f32[8,72,256]{2,1,0:T(8,128)}, f32[8,72,256]{2,1,0:T(8,128)S(1)}, u32[]{:S(2)}, u32[]{:S(2)}) collective-permute-start(f32[8,72,256]{2,1,0:T(8,128)} %get-tuple-element.17), channel_id=1, source_target_pairs={{0,8},{8,0},{16,24},{24,16},{32,40},{40,32},{48,56},{56,48},{64,72... | collective-permute-start | bytes 1769480 | tf_op jit(solution)/shard_map/ppermute | solution.py:409
  18.8 29.4 %all-to-all-start = ((f32[8,72,256]{2,1,0:T(8,128)}), f32[8,72,256]{2,1,0:T(8,128)S(1)}, u32[]{:S(2)}, u32[]{:S(2)}) async-start(f32[8,72,256]{2,1,0:T(8,128)} %add.16.after_ref), calls=%async_computation | async-start | bytes 1179648 | tf_op jit(solution)/shard_map/all_to_all | solution.py:382
  28.8 66.0 %reduce-scatter.3.cloned.1.call-start = ((), (), s32[]{:S(2)}) async-start(), calls=%async_computation.7 | async-start | bytes 3538944 | tf_op jit(solution)/shard_map/reduce_scatter | solution.py:438
  48.2 0.6 copy-start.3
  49.5 17.3 %copy-start.2 = (s32[24]{0:T(128)S(1)}, s32[24]{0:T(128)}, u32[]{:S(2)}) copy-start(s32[24]{0:T(128)} %dynamic-slice_bitcast_fusion.s_ref) | copy-start | bytes 292
  91.3 17.7 %all-to-all-start.4 = ((f32[8,64,256]{2,1,0:T(8,128)}), f32[8,64,256]{2,1,0:T(8,128)S(1)}, u32[]{:S(2)}, u32[]{:S(2)}) async-start(f32[8,64,256]{2,1,0:T(8,128)} %get-tuple-element.24), calls=%async_computation.5 | async-start | bytes 1048576 | tf_op jit(solution)/shard_map/all_to_all | solution.py:382
  94.8 49.8 %reduce-scatter.5.cloned.1.call-start = ((), (), s32[]{:S(2)}) async-start(), calls=%async_computation.8 | async-start | bytes 491520 | tf_op jit(solution)/shard_map/reduce_scatter | solution.py:439
  95.5 23.2 %collective-permute-start.1 = (f32[8,80,256]{2,1,0:T(8,128)}, f32[8,80,256]{2,1,0:T(8,128)S(1)}, u32[]{:S(2)}, u32[]{:S(2)}) collective-permute-start(f32[8,80,256]{2,1,0:T(8,128)} %after.3.mine_ref), channel_id=1, source_target_pairs={{0,8},{8,0},{16,24},{24,16},{32,40},{40,32},{48,56},{56,48},{64,72... | collective-permute-start | bytes 1966088 | tf_op jit(solution)/shard_map/ppermute | solution.py:459
  109.0 27.9 %collective-permute-start.2 = (f32[512,256]{1,0:T(8,128)S(1)}, f32[512,256]{1,0:T(8,128)S(1)}, u32[]{:S(2)}, u32[]{:S(2)}) collective-permute-start(f32[512,256]{1,0:T(8,128)S(1)} %bitcast.4), channel_id=1, source_target_pairs={{3,2},{4,0},{5,1},{6,3},{7,4},{2,5},{0,7},{11,10},{12,8},{13,9},{1... | collective-permute-start | bytes 1572872 | tf_op jit(solution)/shard_map/ppermute | solution.py:460
  112.4 24.4 %collective-permute-start.3 = (f32[512,256]{1,0:T(8,128)S(1)}, f32[512,256]{1,0:T(8,128)S(1)}, u32[]{:S(2)}, u32[]{:S(2)}) collective-permute-start(f32[512,256]{1,0:T(8,128)S(1)} %bitcast.5), channel_id=1, source_target_pairs={{3,4},{4,6},{5,2},{1,0},{7,3},{0,1},{11,12},{12,14},{13,10},{9,8},... | collective-permute-start | bytes 1572872 | tf_op jit(solution)/shard_map/ppermute | solution.py:460
  113.7 30.9 %collective-permute-start.4 = (f32[512,256]{1,0:T(8,128)S(1)}, f32[512,256]{1,0:T(8,128)S(1)}, u32[]{:S(2)}, u32[]{:S(2)}) collective-permute-start(f32[512,256]{1,0:T(8,128)S(1)} %bitcast.6), channel_id=1, source_target_pairs={{3,5},{4,7},{1,2},{2,6},{11,13},{12,15},{9,10},{10,14},{19,21},{20... | collective-permute-start | bytes 1572872 | tf_op jit(solution)/shard_map/ppermute | solution.py:460
  118.8 1.1 copy-start
  144.6 0.9 copy-start.1
  146.8 5.2 %collective-permute-start.5 = (f32[8,1536]{1,0:T(8,128)S(1)}, f32[8,1536]{1,0:T(8,128)S(1)}, u32[]{:S(2)}, u32[]{:S(2)}) collective-permute-start(f32[8,1536]{1,0:T(8,128)S(1)} %get-tuple-element.26), channel_id=1, source_target_pairs={{0,8},{8,0},{16,24},{24,16},{32,40},{40,32},{48,56},{56,48},{64,72... | collective-permute-start | bytes 147464 | tf_op jit(solution)/shard_map/ppermute | solution.py:495
Sparse Core Ops, SparseCore 0:
  49.7 45.0 reduce-scatter.2
  98.5 30.4 reduce-scatter.4

commit v4 on v3

--- a/solution.py
+++ b/solution.py
@@ -159,6 +159,7 @@
         in_specs=[HBM, where],
         out_specs=HBM,
         input_output_aliases={0: 0},
+        cost_estimate=pl.CostEstimate(flops=0, bytes_accessed=0, transcendentals=0),
         name="after",
     )(x, dep)
 
@@ -455,7 +456,6 @@
     column = exchange(held_rows, Z_GROUPS).reshape(BS, HALF)
     share = jnp.concatenate([corner_rows.reshape(64, HALF), own_rows], axis=0)
     share = lax.all_to_all(jnp.broadcast_to(share, (NBLK, 80, HALF)), "blk", 0, 0)
-    share = after(share, rest_z)
     share_other = lax.ppermute(share, "dp", CORE_SWAP)
     brought = [lax.ppermute(column, "blk", list(pairs)) for pairs in ROUNDS]
 

time: 161 us -> 161 us (level)
  no operation moved by 1% of the time
where the time goes in v4:
time: 161 us; the launch traced here: 160 us
  blocking collectives  40.2 us (25%)
  starting transfers between devices  35.5 us (22%)
  waiting for transfers between devices  33.3 us (21%)
  Pallas kernels  32.6 us (20%)
  between operations  13.5 us (8%)
  local copies, waits for them, and re-layouts  2.8 us (2%)
  other arithmetic  1.96 us (1%)
    all_to_all x2, blocking collectives, exchange(): return lax.all_to_all(x, 'dp', 0, 0, axis_index_groups=groups)  28.1 us
    all_to_all x2, waiting for transfers between devices, exchange(): return lax.all_to_all(x, 'dp', 0, 0, axis_index_groups=groups)  21.2 us
    pallas_call x1, Pallas kernels, body(): pl.pallas_call(corner_kernel, out_shape=[jax.ShapeDtypeStruct((16, BS), F...  16.9 us
    all_to_all x2, starting transfers between devices, exchange(): return lax.all_to_all(x, 'dp', 0, 0, axis_index_groups=groups)  13.5 us
    all_to_all x1, blocking collectives, body(): lax.all_to_all(jnp.broadcast_to(share, (NBLK, 80, HALF)), 'blk', 0, 0)  12.1 us
    ppermute x3, starting transfers between devices, body(): brought = [lax.ppermute(column, 'blk', list(pairs)) for pairs in ROUNDS]  9.93 us
    ppermute x3, waiting for transfers between devices, body(): brought = [lax.ppermute(column, 'blk', list(pairs)) for pairs in ROUNDS]  8.75 us
    pallas_call x1, Pallas kernels, body(): pl.pallas_call(trailing_kernel, out_shape=jax.ShapeDtypeStruct((BS, 3 * B...  6.45 us
  transfers between devices with their start and end apart: 10, of which 5 were waited for; matrix products, arithmetic and copies ran while one was open for 0% of the time, Pallas kernels for 15%

profile of v4, /device:TPU:19, one launch (start us, length us, event | category | flops | bytes accessed | tf_op | source)
XLA Modules:
  0.0 159.9 jit_solution(5699994694972861652)
XLA Ops:
  6.5 1.3 dynamic-slice_bitcast_fusion.s_ref
  7.8 4.7 %first_column.1 = (f32[8,72,256]{2,1,0:T(8,128)}, f32[8,72,256]{2,1,0:T(8,128)}) custom-call(s32[24]{0:T(128)} %dynamic-slice_bitcast_fusion.s_ref, bf16[640,3584]{1,0:T(8,128)(2,1)} %aj_ref.1, bf16[640,3584]{1,0:T(8,128)(2,1)} %aj_ref.1), custom_call_target="tpu_custom_call" | custom-call | tf_op jit(solution)/shard_map/first_column/pallas_call | solution.py:394
  12.5 2.6 %collective-permute-start = (f32[8,72,256]{2,1,0:T(8,128)}, f32[8,72,256]{2,1,0:T(8,128)S(1)}, u32[]{:S(2)}, u32[]{:S(2)}) collective-permute-start(f32[8,72,256]{2,1,0:T(8,128)} %get-tuple-element.17), channel_id=1, source_target_pairs={{0,8},{8,0},{16,24},{24,16},{32,40},{40,32},{48,56},{56,48},{64,72... | collective-permute-start | bytes 1769480 | tf_op jit(solution)/shard_map/ppermute | solution.py:410
  15.0 1.8 %collective-permute-done = f32[8,72,256]{2,1,0:T(8,128)S(1)} collective-permute-done((f32[8,72,256]{2,1,0:T(8,128)}, f32[8,72,256]{2,1,0:T(8,128)S(1)}, u32[]{:S(2)}, u32[]{:S(2)}) %collective-permute-start) | collective-permute-done | bytes 589856 | tf_op jit(solution)/shard_map/ppermute | solution.py:410
  16.9 2.0 %add.16.after_ref = f32[8,72,256]{2,1,0:T(8,128)} add(f32[8,72,256]{2,1,0:T(8,128)} %get-tuple-element.16, f32[8,72,256]{2,1,0:T(8,128)S(1)} %collective-permute-done) | non-fusion elementwise | flops 147456 | bytes 1769472 | tf_op jit(solution)/shard_map/add | solution.py:410
  18.8 10.0 %all-to-all-start = ((f32[8,72,256]{2,1,0:T(8,128)}), f32[8,72,256]{2,1,0:T(8,128)S(1)}, u32[]{:S(2)}, u32[]{:S(2)}) async-start(f32[8,72,256]{2,1,0:T(8,128)} %add.16.after_ref), calls=%async_computation | async-start | bytes 1179648 | tf_op jit(solution)/shard_map/all_to_all | solution.py:383
  28.9 0.0 reduce-scatter.3.cloned.1.call-start
  28.9 6.4 %trailing_gram.1.x_ref = f32[512,1536]{1,0:T(8,128)} custom-call(s32[24]{0:T(128)} %dynamic-slice_bitcast_fusion.s_ref, bf16[640,3584]{1,0:T(8,128)(2,1)} %aj_ref.1, bf16[640,3584]{1,0:T(8,128)(2,1)} %aj_ref.1, f32[8,72,256]{2,1,0:T(8,128)} %add.16.after_ref), custom_call_target="tpu_custom_call" | custom-call | flops 4000000000 | bytes 7000000 | tf_op jit(solution)/shard_map/trailing_gram/pallas_call | solution.py:413
  35.3 12.9 %all-to-all-done.x_ref = f32[8,72,256]{2,1,0:T(8,128)S(1)} async-done(((f32[8,72,256]{2,1,0:T(8,128)}), f32[8,72,256]{2,1,0:T(8,128)S(1)}, u32[]{:S(2)}, u32[]{:S(2)}) %all-to-all-start) | async-done | bytes 589856 | tf_op jit(solution)/shard_map/all_to_all | solution.py:383
  48.3 0.6 copy-done.2
  48.8 0.7 after.1
  49.5 0.0 reduce-scatter.3.cloned.1.call-update
  49.6 17.3 %all_to_all.25.x_ref = f32[4,72,256]{2,1,0:T(8,128)S(1)} all-to-all(f32[4,72,256]{2,1,0:T(8,128)S(1)} %get-tuple-element.18), channel_id=1, replica_groups={{0,16,32,48},{8,24,40,56},{64,80,96,112},{72,88,104,120},{128,144,160,1..., dimensions={0} | all-to-all | bytes 589824 | tf_op jit(solution)/shard_map/all_to_all | solution.py:383
  66.8 1.4 sum_over_y.1
  68.3 10.8 %all_to_all.26 = f32[8,8,256]{2,1,0:T(8,128)S(1)} all-to-all(f32[8,8,256]{2,1,0:T(8,128)S(1)} %get-tuple-element.19), channel_id=1, replica_groups={{0,64,128,192,256,320,384,448},{8,72,136,200,264,328,392,456},{16,80,14..., dimensions={0} | all-to-all | bytes 131072 | tf_op jit(solution)/shard_map/all_to_all | solution.py:383
  79.1 12.1 %all_to_all.27.mine_ref = f32[8,80,256]{2,1,0:T(8,128)S(1)} all-to-all(f32[8,80,256]{2,1,0:T(8,128)S(1)} %broadcast_in_dim.3), channel_id=1, replica_groups=mesh['dp'=64,'blk'=8] {'blk'}, dimensions={0} | all-to-all | bytes 1310720 | tf_op jit(solution)/shard_map/all_to_all | solution.py:458
  91.2 3.5 %all-to-all-start.4 = ((f32[8,64,256]{2,1,0:T(8,128)}), f32[8,64,256]{2,1,0:T(8,128)S(1)}, u32[]{:S(2)}, u32[]{:S(2)}) async-start(f32[8,64,256]{2,1,0:T(8,128)} %get-tuple-element.23), calls=%async_computation.4 | async-start | bytes 1048576 | tf_op jit(solution)/shard_map/all_to_all | solution.py:383
  94.7 0.0 reduce-scatter.5.cloned.1.call-start
  94.8 0.0 reduce-scatter.3.cloned.1.call-done
  94.8 0.7 reduce-scatter.5.cloned.1.call-update
  95.5 5.1 %collective-permute-start.1 = (f32[8,80,256]{2,1,0:T(8,128)S(1)}, f32[8,80,256]{2,1,0:T(8,128)S(1)}, u32[]{:S(2)}, u32[]{:S(2)}) collective-permute-start(f32[8,80,256]{2,1,0:T(8,128)S(1)} %all_to_all.27.mine_ref), channel_id=1, source_target_pairs={{0,8},{8,0},{16,24},{24,16},{32,40},{40,32},{48,56},{56,48},{64,72... | collective-permute-start | bytes 1966088 | tf_op jit(solution)/shard_map/ppermute | solution.py:459
  100.6 8.3 %all-to-all-done.4 = f32[8,64,256]{2,1,0:T(8,128)S(1)} async-done(((f32[8,64,256]{2,1,0:T(8,128)}), f32[8,64,256]{2,1,0:T(8,128)S(1)}, u32[]{:S(2)}, u32[]{:S(2)}) %all-to-all-start.4) | async-done | bytes 524320 | tf_op jit(solution)/shard_map/all_to_all | solution.py:383
  108.9 3.7 %collective-permute-start.2 = (f32[512,256]{1,0:T(8,128)S(1)}, f32[512,256]{1,0:T(8,128)S(1)}, u32[]{:S(2)}, u32[]{:S(2)}) collective-permute-start(f32[512,256]{1,0:T(8,128)S(1)} %bitcast.4), channel_id=1, source_target_pairs={{3,2},{4,0},{5,1},{6,3},{7,4},{2,5},{0,7},{11,10},{12,8},{13,9},{1... | collective-permute-start | bytes 1572872 | tf_op jit(solution)/shard_map/ppermute | solution.py:460
  112.6 1.3 collective-permute-start.3
  113.9 5.0 %collective-permute-start.4 = (f32[512,256]{1,0:T(8,128)S(1)}, f32[512,256]{1,0:T(8,128)S(1)}, u32[]{:S(2)}, u32[]{:S(2)}) collective-permute-start(f32[512,256]{1,0:T(8,128)S(1)} %bitcast.6), channel_id=1, source_target_pairs={{3,5},{4,7},{1,2},{2,6},{11,13},{12,15},{9,10},{10,14},{19,21},{20... | collective-permute-start | bytes 1572872 | tf_op jit(solution)/shard_map/ppermute | solution.py:460
  118.9 16.9 %corner.1 = (f32[16,512]{1,0:T(8,128)S(1)}, f32[48,256]{1,0:T(8,128)S(1)}) custom-call(s32[24]{0:T(128)S(1)} %copy-done.1, f32[8,80,256]{2,1,0:T(8,128)S(1)} %all_to_all.27.mine_ref, f32[8,80,256]{2,1,0:T(8,128)S(1)} %collective-permute-done.1.other_ref), custom_call_target="tpu_custom_call" | custom-call | flops 200000000 | bytes 2000000 | tf_op jit(solution)/shard_map/corner/pallas_call | solution.py:462
  135.8 8.7 %collective-permute-done.4.r2_ref = f32[512,256]{1,0:T(8,128)S(1)} collective-permute-done((f32[512,256]{1,0:T(8,128)S(1)}, f32[512,256]{1,0:T(8,128)S(1)}, u32[]{:S(2)}, u32[]{:S(2)}) %collective-permute-start.4) | collective-permute-done | bytes 524320 | tf_op jit(solution)/shard_map/ppermute | solution.py:460
  144.6 0.9 copy-done
  145.5 1.3 update.1
  146.7 4.3 %collective-permute-start.5 = (f32[8,1536]{1,0:T(8,128)S(1)}, f32[8,1536]{1,0:T(8,128)S(1)}, u32[]{:S(2)}, u32[]{:S(2)}) collective-permute-start(f32[8,1536]{1,0:T(8,128)S(1)} %get-tuple-element.26), channel_id=1, source_target_pairs={{0,8},{8,0},{16,24},{24,16},{32,40},{40,32},{48,56},{56,48},{64,72... | collective-permute-start | bytes 147464 | tf_op jit(solution)/shard_map/ppermute | solution.py:495
  151.0 0.9 collective-permute-done.5.other_ref
  151.9 1.2 finish.1
  (11 shorter events, 0.1 us)
Async XLA Ops:
  12.5 4.4 %collective-permute-start = (f32[8,72,256]{2,1,0:T(8,128)}, f32[8,72,256]{2,1,0:T(8,128)S(1)}, u32[]{:S(2)}, u32[]{:S(2)}) collective-permute-start(f32[8,72,256]{2,1,0:T(8,128)} %get-tuple-element.17), channel_id=1, source_target_pairs={{0,8},{8,0},{16,24},{24,16},{32,40},{40,32},{48,56},{56,48},{64,72... | collective-permute-start | bytes 1769480 | tf_op jit(solution)/shard_map/ppermute | solution.py:410
  18.8 29.4 %all-to-all-start = ((f32[8,72,256]{2,1,0:T(8,128)}), f32[8,72,256]{2,1,0:T(8,128)S(1)}, u32[]{:S(2)}, u32[]{:S(2)}) async-start(f32[8,72,256]{2,1,0:T(8,128)} %add.16.after_ref), calls=%async_computation | async-start | bytes 1179648 | tf_op jit(solution)/shard_map/all_to_all | solution.py:383
  28.9 65.9 %reduce-scatter.3.cloned.1.call-start = ((), (), s32[]{:S(2)}) async-start(), calls=%async_computation.7 | async-start | bytes 3538944 | tf_op jit(solution)/shard_map/reduce_scatter | solution.py:439
  48.3 0.6 copy-start.2
  49.5 17.3 %copy-start.1 = (s32[24]{0:T(128)S(1)}, s32[24]{0:T(128)}, u32[]{:S(2)}) copy-start(s32[24]{0:T(128)} %dynamic-slice_bitcast_fusion.s_ref) | copy-start | bytes 292
  91.2 17.7 %all-to-all-start.4 = ((f32[8,64,256]{2,1,0:T(8,128)}), f32[8,64,256]{2,1,0:T(8,128)S(1)}, u32[]{:S(2)}, u32[]{:S(2)}) async-start(f32[8,64,256]{2,1,0:T(8,128)} %get-tuple-element.23), calls=%async_computation.4 | async-start | bytes 1048576 | tf_op jit(solution)/shard_map/all_to_all | solution.py:383
  94.7 49.8 %reduce-scatter.5.cloned.1.call-start = ((), (), s32[]{:S(2)}) async-start(), calls=%async_computation.8 | async-start | bytes 491520 | tf_op jit(solution)/shard_map/reduce_scatter | solution.py:440
  95.5 23.4 %collective-permute-start.1 = (f32[8,80,256]{2,1,0:T(8,128)S(1)}, f32[8,80,256]{2,1,0:T(8,128)S(1)}, u32[]{:S(2)}, u32[]{:S(2)}) collective-permute-start(f32[8,80,256]{2,1,0:T(8,128)S(1)} %all_to_all.27.mine_ref), channel_id=1, source_target_pairs={{0,8},{8,0},{16,24},{24,16},{32,40},{40,32},{48,56},{56,48},{64,72... | collective-permute-start | bytes 1966088 | tf_op jit(solution)/shard_map/ppermute | solution.py:459
  108.9 26.9 %collective-permute-start.2 = (f32[512,256]{1,0:T(8,128)S(1)}, f32[512,256]{1,0:T(8,128)S(1)}, u32[]{:S(2)}, u32[]{:S(2)}) collective-permute-start(f32[512,256]{1,0:T(8,128)S(1)} %bitcast.4), channel_id=1, source_target_pairs={{3,2},{4,0},{5,1},{6,3},{7,4},{2,5},{0,7},{11,10},{12,8},{13,9},{1... | collective-permute-start | bytes 1572872 | tf_op jit(solution)/shard_map/ppermute | solution.py:460
  112.6 23.2 %collective-permute-start.3 = (f32[512,256]{1,0:T(8,128)S(1)}, f32[512,256]{1,0:T(8,128)S(1)}, u32[]{:S(2)}, u32[]{:S(2)}) collective-permute-start(f32[512,256]{1,0:T(8,128)S(1)} %bitcast.5), channel_id=1, source_target_pairs={{3,4},{4,6},{5,2},{1,0},{7,3},{0,1},{11,12},{12,14},{13,10},{9,8},... | collective-permute-start | bytes 1572872 | tf_op jit(solution)/shard_map/ppermute | solution.py:460
  113.9 30.7 %collective-permute-start.4 = (f32[512,256]{1,0:T(8,128)S(1)}, f32[512,256]{1,0:T(8,128)S(1)}, u32[]{:S(2)}, u32[]{:S(2)}) collective-permute-start(f32[512,256]{1,0:T(8,128)S(1)} %bitcast.6), channel_id=1, source_target_pairs={{3,5},{4,7},{1,2},{2,6},{11,13},{12,15},{9,10},{10,14},{19,21},{20... | collective-permute-start | bytes 1572872 | tf_op jit(solution)/shard_map/ppermute | solution.py:460
  144.6 0.9 copy-start
  146.7 5.2 %collective-permute-start.5 = (f32[8,1536]{1,0:T(8,128)S(1)}, f32[8,1536]{1,0:T(8,128)S(1)}, u32[]{:S(2)}, u32[]{:S(2)}) collective-permute-start(f32[8,1536]{1,0:T(8,128)S(1)} %get-tuple-element.26), channel_id=1, source_target_pairs={{0,8},{8,0},{16,24},{24,16},{32,40},{40,32},{48,56},{56,48},{64,72... | collective-permute-start | bytes 147464 | tf_op jit(solution)/shard_map/ppermute | solution.py:495
Sparse Core Ops, SparseCore 0:
  49.7 45.0 reduce-scatter.2
  98.4 30.4 reduce-scatter.4

commit v5 on v4

--- a/solution.py
+++ b/solution.py
@@ -404,7 +404,7 @@
             out_specs=[pl.BlockSpec((NZ, 72, HALF), lambda g, s: (0, 0, 0))] * 2,
             scratch_shapes=[pltpu.VMEM((BS, BS), F32)],
         ),
-        compiler_params=params(GRAM_LIMIT),
+        compiler_params=params(),
         name="first_column",
     )(place, act, act)
     first = mine + lax.ppermute(other, "dp", CORE_SWAP)

time: 161 us -> 159 us (0.988)
  Pallas kernels: 32.6 us -> 30.1 us
  local copies, waits for them, and re-layouts: 2.8 us -> 4.53 us
    pallas_call x1, Pallas kernels: 4.66 us -> 2.19 us  [body(): pl.pallas_call(first_column_kernel, out_shape=[piece, piece], grid_spec=p...]
    unnamed x6 -> x10, local copies, waits for them, and re-layouts: 1.48 us -> 3.79 us
  transfers between devices with their start and end apart: 10 -> 10, of which waited for: 5 -> 5; matrix products, arithmetic and copies ran while one was open for 0% -> 0% of each run, Pallas kernels for 15% -> 16%
where the time goes in v5:
time: 159 us; the launch traced here: 158 us
  blocking collectives  40.1 us (25%)
  starting transfers between devices  35.7 us (22%)
  waiting for transfers between devices  32.9 us (21%)
  Pallas kernels  30.1 us (19%)
  between operations  13.5 us (8%)
  local copies, waits for them, and re-layouts  4.53 us (3%)
    all_to_all x2, blocking collectives, exchange(): return lax.all_to_all(x, 'dp', 0, 0, axis_index_groups=groups)  28.1 us
    all_to_all x2, waiting for transfers between devices, exchange(): return lax.all_to_all(x, 'dp', 0, 0, axis_index_groups=groups)  21.2 us
    pallas_call x1, Pallas kernels, body(): pl.pallas_call(corner_kernel, out_shape=[jax.ShapeDtypeStruct((16, BS), F...  16.9 us
    all_to_all x2, starting transfers between devices, exchange(): return lax.all_to_all(x, 'dp', 0, 0, axis_index_groups=groups)  13.5 us
    all_to_all x1, blocking collectives, body(): lax.all_to_all(jnp.broadcast_to(share, (NBLK, 80, HALF)), 'blk', 0, 0)  12.1 us
    ppermute x3, starting transfers between devices, body(): brought = [lax.ppermute(column, 'blk', list(pairs)) for pairs in ROUNDS]  9.94 us
    ppermute x3, waiting for transfers between devices, body(): brought = [lax.ppermute(column, 'blk', list(pairs)) for pairs in ROUNDS]  8.53 us
    pallas_call x1, Pallas kernels, body(): pl.pallas_call(trailing_kernel, out_shape=jax.ShapeDtypeStruct((BS, 3 * B...  6.44 us
  transfers between devices with their start and end apart: 10, of which 5 were waited for; matrix products, arithmetic and copies ran while one was open for 0% of the time, Pallas kernels for 16%

profile of v5, /device:TPU:19, one launch (start us, length us, event | category | flops | bytes accessed | tf_op | source)
XLA Modules:
  0.0 157.9 jit_solution(3535830490846826484)
XLA Ops:
  6.5 0.7 dynamic-slice_bitcast_fusion.s_ref
  7.2 2.3 %copy-done = bf16[640,3584]{1,0:T(8,128)(2,1)S(1)} copy-done((bf16[640,3584]{1,0:T(8,128)(2,1)S(1)}, bf16[640,3584]{1,0:T(8,128)(2,1)}, u32[]{:S(2)}) %copy-start) | copy-done | bytes 4587544
  9.5 2.2 %first_column.1 = (f32[8,72,256]{2,1,0:T(8,128)S(1)}, f32[8,72,256]{2,1,0:T(8,128)S(1)}) custom-call(s32[24]{0:T(128)S(1)} %dynamic-slice_bitcast_fusion.s_ref, bf16[640,3584]{1,0:T(8,128)(2,1)S(1)} %copy-done, bf16[640,3584]{1,0:T(8,128)(2,1)S(1)} %copy-done), custom_call_target="tpu_custom_call" | custom-call | tf_op jit(solution)/shard_map/first_column/pallas_call | solution.py:394
  11.7 2.6 %collective-permute-start = (f32[8,72,256]{2,1,0:T(8,128)S(1)}, f32[8,72,256]{2,1,0:T(8,128)S(1)}, u32[]{:S(2)}, u32[]{:S(2)}) collective-permute-start(f32[8,72,256]{2,1,0:T(8,128)S(1)} %get-tuple-element.17), channel_id=1, source_target_pairs={{0,8},{8,0},{16,24},{24,16},{32,40},{40,32},{48,56},{56,48},{64,72... | collective-permute-start | bytes 1769480 | tf_op jit(solution)/shard_map/ppermute | solution.py:410
  14.3 1.6 %collective-permute-done = f32[8,72,256]{2,1,0:T(8,128)S(1)} collective-permute-done((f32[8,72,256]{2,1,0:T(8,128)S(1)}, f32[8,72,256]{2,1,0:T(8,128)S(1)}, u32[]{:S(2)}, u32[]{:S(2)}) %collective-permute-start) | collective-permute-done | bytes 589856 | tf_op jit(solution)/shard_map/ppermute | solution.py:410
  15.9 0.9 add.16.after_ref
  16.8 10.0 %all-to-all-start = ((f32[8,72,256]{2,1,0:T(8,128)}), f32[8,72,256]{2,1,0:T(8,128)S(1)}, u32[]{:S(2)}, u32[]{:S(2)}) async-start(f32[8,72,256]{2,1,0:T(8,128)} %add.16.after_ref), calls=%async_computation | async-start | bytes 1179648 | tf_op jit(solution)/shard_map/all_to_all | solution.py:383
  26.9 0.0 reduce-scatter.3.cloned.1.call-start
  26.9 6.4 %trailing_gram.1.x_ref = f32[512,1536]{1,0:T(8,128)} custom-call(s32[24]{0:T(128)} %copy-done.2, bf16[640,3584]{1,0:T(8,128)(2,1)} %aj_ref.1, bf16[640,3584]{1,0:T(8,128)(2,1)} %aj_ref.1, f32[8,72,256]{2,1,0:T(8,128)} %add.16.after_ref), custom_call_target="tpu_custom_call" | custom-call | flops 4000000000 | bytes 7000000 | tf_op jit(solution)/shard_map/trailing_gram/pallas_call | solution.py:413
  33.4 12.9 %all-to-all-done.x_ref = f32[8,72,256]{2,1,0:T(8,128)S(1)} async-done(((f32[8,72,256]{2,1,0:T(8,128)}), f32[8,72,256]{2,1,0:T(8,128)S(1)}, u32[]{:S(2)}, u32[]{:S(2)}) %all-to-all-start) | async-done | bytes 589856 | tf_op jit(solution)/shard_map/all_to_all | solution.py:383
  46.3 0.6 copy-done.4
  46.9 0.7 after.1
  47.6 17.3 %all_to_all.25.x_ref = f32[4,72,256]{2,1,0:T(8,128)S(1)} all-to-all(f32[4,72,256]{2,1,0:T(8,128)S(1)} %get-tuple-element.18), channel_id=1, replica_groups={{0,16,32,48},{8,24,40,56},{64,80,96,112},{72,88,104,120},{128,144,160,1..., dimensions={0} | all-to-all | bytes 589824 | tf_op jit(solution)/shard_map/all_to_all | solution.py:383
  64.9 1.4 sum_over_y.1
  66.3 10.8 %all_to_all.26 = f32[8,8,256]{2,1,0:T(8,128)S(1)} all-to-all(f32[8,8,256]{2,1,0:T(8,128)S(1)} %get-tuple-element.19), channel_id=1, replica_groups={{0,64,128,192,256,320,384,448},{8,72,136,200,264,328,392,456},{16,80,14..., dimensions={0} | all-to-all | bytes 131072 | tf_op jit(solution)/shard_map/all_to_all | solution.py:383
  77.1 12.1 %all_to_all.27.mine_ref = f32[8,80,256]{2,1,0:T(8,128)S(1)} all-to-all(f32[8,80,256]{2,1,0:T(8,128)S(1)} %broadcast_in_dim.3), channel_id=1, replica_groups=mesh['dp'=64,'blk'=8] {'blk'}, dimensions={0} | all-to-all | bytes 1310720 | tf_op jit(solution)/shard_map/all_to_all | solution.py:458
  89.2 3.5 %all-to-all-start.4 = ((f32[8,64,256]{2,1,0:T(8,128)}), f32[8,64,256]{2,1,0:T(8,128)S(1)}, u32[]{:S(2)}, u32[]{:S(2)}) async-start(f32[8,64,256]{2,1,0:T(8,128)} %get-tuple-element.23), calls=%async_computation.4 | async-start | bytes 1048576 | tf_op jit(solution)/shard_map/all_to_all | solution.py:383
  92.7 0.0 reduce-scatter.5.cloned.1.call-start
  92.8 0.0 reduce-scatter.3.cloned.1.call-done
  92.8 0.7 reduce-scatter.5.cloned.1.call-update
  93.5 5.1 %collective-permute-start.1 = (f32[8,80,256]{2,1,0:T(8,128)S(1)}, f32[8,80,256]{2,1,0:T(8,128)S(1)}, u32[]{:S(2)}, u32[]{:S(2)}) collective-permute-start(f32[8,80,256]{2,1,0:T(8,128)S(1)} %all_to_all.27.mine_ref), channel_id=1, source_target_pairs={{0,8},{8,0},{16,24},{24,16},{32,40},{40,32},{48,56},{56,48},{64,72... | collective-permute-start | bytes 1966088 | tf_op jit(solution)/shard_map/ppermute | solution.py:459
  98.6 8.3 %all-to-all-done.4 = f32[8,64,256]{2,1,0:T(8,128)S(1)} async-done(((f32[8,64,256]{2,1,0:T(8,128)}), f32[8,64,256]{2,1,0:T(8,128)S(1)}, u32[]{:S(2)}, u32[]{:S(2)}) %all-to-all-start.4) | async-done | bytes 524320 | tf_op jit(solution)/shard_map/all_to_all | solution.py:383
  106.9 3.7 %collective-permute-start.2 = (f32[512,256]{1,0:T(8,128)S(1)}, f32[512,256]{1,0:T(8,128)S(1)}, u32[]{:S(2)}, u32[]{:S(2)}) collective-permute-start(f32[512,256]{1,0:T(8,128)S(1)} %bitcast.4), channel_id=1, source_target_pairs={{3,2},{4,0},{5,1},{6,3},{7,4},{2,5},{0,7},{11,10},{12,8},{13,9},{1... | collective-permute-start | bytes 1572872 | tf_op jit(solution)/shard_map/ppermute | solution.py:460
  110.6 1.3 collective-permute-start.3
  111.9 5.0 %collective-permute-start.4 = (f32[512,256]{1,0:T(8,128)S(1)}, f32[512,256]{1,0:T(8,128)S(1)}, u32[]{:S(2)}, u32[]{:S(2)}) collective-permute-start(f32[512,256]{1,0:T(8,128)S(1)} %bitcast.6), channel_id=1, source_target_pairs={{3,5},{4,7},{1,2},{2,6},{11,13},{12,15},{9,10},{10,14},{19,21},{20... | collective-permute-start | bytes 1572872 | tf_op jit(solution)/shard_map/ppermute | solution.py:460
  116.9 16.9 %corner.1 = (f32[16,512]{1,0:T(8,128)S(1)}, f32[48,256]{1,0:T(8,128)S(1)}) custom-call(s32[24]{0:T(128)S(1)} %copy-done.3, f32[8,80,256]{2,1,0:T(8,128)S(1)} %all_to_all.27.mine_ref, f32[8,80,256]{2,1,0:T(8,128)S(1)} %collective-permute-done.1.other_ref), custom_call_target="tpu_custom_call" | custom-call | flops 200000000 | bytes 2000000 | tf_op jit(solution)/shard_map/corner/pallas_call | solution.py:462
  133.8 8.5 %collective-permute-done.4.r2_ref = f32[512,256]{1,0:T(8,128)S(1)} collective-permute-done((f32[512,256]{1,0:T(8,128)S(1)}, f32[512,256]{1,0:T(8,128)S(1)}, u32[]{:S(2)}, u32[]{:S(2)}) %collective-permute-start.4) | collective-permute-done | bytes 524320 | tf_op jit(solution)/shard_map/ppermute | solution.py:460
  142.3 0.9 copy-done.1
  143.2 1.3 update.1
  144.5 4.5 %collective-permute-start.5 = (f32[8,1536]{1,0:T(8,128)S(1)}, f32[8,1536]{1,0:T(8,128)S(1)}, u32[]{:S(2)}, u32[]{:S(2)}) collective-permute-start(f32[8,1536]{1,0:T(8,128)S(1)} %get-tuple-element.26), channel_id=1, source_target_pairs={{0,8},{8,0},{16,24},{24,16},{32,40},{40,32},{48,56},{56,48},{64,72... | collective-permute-start | bytes 147464 | tf_op jit(solution)/shard_map/ppermute | solution.py:495
  149.0 0.9 collective-permute-done.5.other_ref
  149.9 1.2 finish.1
  (15 shorter events, 0.1 us)
Async XLA Ops:
  7.2 2.3 %copy-start = (bf16[640,3584]{1,0:T(8,128)(2,1)S(1)}, bf16[640,3584]{1,0:T(8,128)(2,1)}, u32[]{:S(2)}) copy-start(bf16[640,3584]{1,0:T(8,128)(2,1)} %aj_ref.1) | copy-start | bytes 13762564
  9.5 2.2 %copy-start.2 = (s32[24]{0:T(128)}, s32[24]{0:T(128)S(1)}, u32[]{:S(2)}) copy-start(s32[24]{0:T(128)S(1)} %dynamic-slice_bitcast_fusion.s_ref) | copy-start | bytes 292
  11.7 4.2 %collective-permute-start = (f32[8,72,256]{2,1,0:T(8,128)S(1)}, f32[8,72,256]{2,1,0:T(8,128)S(1)}, u32[]{:S(2)}, u32[]{:S(2)}) collective-permute-start(f32[8,72,256]{2,1,0:T(8,128)S(1)} %get-tuple-element.17), channel_id=1, source_target_pairs={{0,8},{8,0},{16,24},{24,16},{32,40},{40,32},{48,56},{56,48},{64,72... | collective-permute-start | bytes 1769480 | tf_op jit(solution)/shard_map/ppermute | solution.py:410
  16.8 29.4 %all-to-all-start = ((f32[8,72,256]{2,1,0:T(8,128)}), f32[8,72,256]{2,1,0:T(8,128)S(1)}, u32[]{:S(2)}, u32[]{:S(2)}) async-start(f32[8,72,256]{2,1,0:T(8,128)} %add.16.after_ref), calls=%async_computation | async-start | bytes 1179648 | tf_op jit(solution)/shard_map/all_to_all | solution.py:383
  26.9 65.9 %reduce-scatter.3.cloned.1.call-start = ((), (), s32[]{:S(2)}) async-start(), calls=%async_computation.7 | async-start | bytes 3538944 | tf_op jit(solution)/shard_map/reduce_scatter | solution.py:439
  46.3 0.6 copy-start.4
  47.6 17.3 %copy-start.3 = (s32[24]{0:T(128)S(1)}, s32[24]{0:T(128)}, u32[]{:S(2)}) copy-start(s32[24]{0:T(128)} %copy-done.2) | copy-start | bytes 292
  89.2 17.7 %all-to-all-start.4 = ((f32[8,64,256]{2,1,0:T(8,128)}), f32[8,64,256]{2,1,0:T(8,128)S(1)}, u32[]{:S(2)}, u32[]{:S(2)}) async-start(f32[8,64,256]{2,1,0:T(8,128)} %get-tuple-element.23), calls=%async_computation.4 | async-start | bytes 1048576 | tf_op jit(solution)/shard_map/all_to_all | solution.py:383
  92.7 49.6 %reduce-scatter.5.cloned.1.call-start = ((), (), s32[]{:S(2)}) async-start(), calls=%async_computation.8 | async-start | bytes 491520 | tf_op jit(solution)/shard_map/reduce_scatter | solution.py:440
  93.5 23.4 %collective-permute-start.1 = (f32[8,80,256]{2,1,0:T(8,128)S(1)}, f32[8,80,256]{2,1,0:T(8,128)S(1)}, u32[]{:S(2)}, u32[]{:S(2)}) collective-permute-start(f32[8,80,256]{2,1,0:T(8,128)S(1)} %all_to_all.27.mine_ref), channel_id=1, source_target_pairs={{0,8},{8,0},{16,24},{24,16},{32,40},{40,32},{48,56},{56,48},{64,72... | collective-permute-start | bytes 1966088 | tf_op jit(solution)/shard_map/ppermute | solution.py:459
  106.9 26.9 %collective-permute-start.2 = (f32[512,256]{1,0:T(8,128)S(1)}, f32[512,256]{1,0:T(8,128)S(1)}, u32[]{:S(2)}, u32[]{:S(2)}) collective-permute-start(f32[512,256]{1,0:T(8,128)S(1)} %bitcast.4), channel_id=1, source_target_pairs={{3,2},{4,0},{5,1},{6,3},{7,4},{2,5},{0,7},{11,10},{12,8},{13,9},{1... | collective-permute-start | bytes 1572872 | tf_op jit(solution)/shard_map/ppermute | solution.py:460
  110.6 23.2 %collective-permute-start.3 = (f32[512,256]{1,0:T(8,128)S(1)}, f32[512,256]{1,0:T(8,128)S(1)}, u32[]{:S(2)}, u32[]{:S(2)}) collective-permute-start(f32[512,256]{1,0:T(8,128)S(1)} %bitcast.5), channel_id=1, source_target_pairs={{3,4},{4,6},{5,2},{1,0},{7,3},{0,1},{11,12},{12,14},{13,10},{9,8},... | collective-permute-start | bytes 1572872 | tf_op jit(solution)/shard_map/ppermute | solution.py:460
  111.9 30.5 %collective-permute-start.4 = (f32[512,256]{1,0:T(8,128)S(1)}, f32[512,256]{1,0:T(8,128)S(1)}, u32[]{:S(2)}, u32[]{:S(2)}) collective-permute-start(f32[512,256]{1,0:T(8,128)S(1)} %bitcast.6), channel_id=1, source_target_pairs={{3,5},{4,7},{1,2},{2,6},{11,13},{12,15},{9,10},{10,14},{19,21},{20... | collective-permute-start | bytes 1572872 | tf_op jit(solution)/shard_map/ppermute | solution.py:460
  142.3 0.9 copy-start.1
  144.5 5.4 %collective-permute-start.5 = (f32[8,1536]{1,0:T(8,128)S(1)}, f32[8,1536]{1,0:T(8,128)S(1)}, u32[]{:S(2)}, u32[]{:S(2)}) collective-permute-start(f32[8,1536]{1,0:T(8,128)S(1)} %get-tuple-element.26), channel_id=1, source_target_pairs={{0,8},{8,0},{16,24},{24,16},{32,40},{40,32},{48,56},{56,48},{64,72... | collective-permute-start | bytes 147464 | tf_op jit(solution)/shard_map/ppermute | solution.py:495
Sparse Core Ops, SparseCore 0:
  47.7 45.0 reduce-scatter.2
  96.4 30.6 reduce-scatter.4
